TPU v7x, 256 devices: a whole 4x4x8 slice. The times are simulated.
256 devices in a mesh: replica: 32 (over y, x, core), tensor: 8 (over z).
Axes of the slice: x: 4, y: 4, z: 8, core: 2. Of those that a mesh axis runs over, the one named last changes fastest.
Arguments:
- normed_token_input: bfloat16 [8192, 2, 8192], P('replica', None, 'tensor'), may hold values from -6 to 6
- rotated_base_query: bfloat16 [8192, 2, 8192], P('replica', None, 'tensor')
- key_value_weight: bfloat16 [8192, 2, 1024], P(None, None, 'tensor'), may hold values from -0.0625 to 0.0625
- key_value_cache: bfloat16 [8192, 2, 32, 1024], P('replica', None, None, 'tensor')
- adapter_down_maps: bfloat16 [128, 192, 8192], P('replica', None, 'tensor'), may hold values from -0.0625 to 0.0625
- query_up_maps: bfloat16 [128, 64, 8192], P('replica', None, 'tensor'), may hold values from -0.75 to 0.75
- key_value_up_maps: bfloat16 [128, 2, 64, 1024], P('replica', None, None, 'tensor'), may hold values from -0.75 to 0.75
- adapter_storage_row: int32 [128], replicated, may hold values from 0 to 127, as said below
- segment_adapter: int32 [512], replicated, may hold values from 0 to 127, as said below
- segment_live_requests: int32 [512], P('replica'), may hold values from 1 to 16, as said below
- cache_length: int32 [8192], P('replica'), may hold values from 2 to 32
Outputs:
- attention: bfloat16 [8192, 2, 8192], P('replica', None, 'tensor')
Inputs may be any that keep to these rules, and one draw needn't show every extreme that they name: Adapter a is stored at row adapter_storage_row[a] of adapter_down_maps, query_up_maps and key_value_up_maps; every row once; rows k * 4 to (k + 1) * 4 - 1 form owner group k. `segment_adapter`: segments s * 16 to (s + 1) * 16 - 1 belong to replica s; the segments of one replica use adapters of different owner groups. The first segment_live_requests[s] request slots of segment s are live, the rest are padding.
All inputs are finite; a program needn't handle non-finite values.
Results may differ from a plain program's by a relative error of at most 0.0066.
Values may be sent and summed in bfloat16 or wider, within the bound.
A program may use at most 192 MiB of HBM per device.

v0:
```python
import math

import jax
import jax.numpy as jnp
from jax import lax
from jax.sharding import PartitionSpec as P

HEAD_WIDTH = 128
CTX = 32


ADAPTER_SCALE = 0.5


def shards(
    normed_token_input,
    rotated_base_query,
    key_value_weight,
    key_value_cache,
    adapter_down_maps,
    query_up_maps,
    key_value_up_maps,
    adapter_storage_row,
    segment_adapter,
    segment_live_requests,
    cache_length,
):
    request_list, token_rows, feature_part = normed_token_input.shape
    head_column_span = key_value_weight.shape[2]
    query_column_span = rotated_base_query.shape[2]
    owning_rows = adapter_down_maps.shape[0]
    rank_portion = adapter_down_maps.shape[1] // 3
    replicas = lax.axis_size("replica")
    segments = segment_live_requests.shape[0]
    seg_size = request_list // segments
    seg_rows = seg_size * token_rows
    adapters = adapter_storage_row.shape[0]
    position = lax.axis_index("replica")
    portion = lax.all_gather(normed_token_input, "tensor", axis=2, tiled=True)
    portion_width = portion.shape[2]
    base_kv = jnp.dot(
        portion.reshape(-1, portion_width),
        key_value_weight.reshape(portion_width, 2 * head_column_span),
        preferred_element_type=jnp.float32,
    )
    adapter_ids = jnp.arange(adapters, dtype=jnp.int32)
    every_slot = jnp.sum(
        jnp.where(
            segment_adapter[:, None] == adapter_ids[None, :], adapter_storage_row[None, :], 0
        ),
        axis=1,
    )
    every_group = (every_slot // owning_rows).reshape(replicas, segments)
    every_local = (every_slot % owning_rows).reshape(replicas, segments)
    local_groups = lax.dynamic_index_in_dim(every_group, position, 0, keepdims=False)
    group_ids = jnp.arange(replicas, dtype=jnp.int32)
    picker = (local_groups[:, None] == group_ids[None, :]).astype(jnp.bfloat16)
    served = every_group == position
    served_local = jnp.sum(jnp.where(served, every_local, 0), axis=1)
    served_any = jnp.any(served, axis=1)
    offered_rows = (
        (served_local[:, None] == jnp.arange(owning_rows, dtype=jnp.int32)[None, :])
        & served_any[:, None]
    ).astype(jnp.bfloat16)
    own_down = jnp.einsum(
        "nu,uwt->nwt", offered_rows, adapter_down_maps, preferred_element_type=jnp.float32
    ).astype(jnp.bfloat16)
    own_query = jnp.einsum(
        "ro,ock->rck", offered_rows, query_up_maps, preferred_element_type=jnp.float32
    ).astype(jnp.bfloat16)
    own_kv = jnp.einsum(
        "ro,otck->rtck", offered_rows, key_value_up_maps, preferred_element_type=jnp.float32
    ).astype(jnp.bfloat16)
    seg_inputs = normed_token_input.reshape(segments, seg_rows, feature_part)
    outgoing = jnp.einsum(
        "sg,smd->gmd", picker, seg_inputs, preferred_element_type=jnp.float32
    ).astype(jnp.bfloat16)[:, None]
    partial_value = jnp.einsum(
        "rmd,rcd->rmc",
        lax.all_to_all(outgoing, "replica", split_axis=0, concat_axis=1, tiled=True)[0],
        own_down,
        preferred_element_type=jnp.float32,
    )
    shrink = lax.psum(partial_value, "tensor").astype(jnp.bfloat16)
    upd_query = jnp.einsum(
        "rmc,rck->rmk", shrink[:, :, :rank_portion], own_query, preferred_element_type=jnp.float32
    ).astype(jnp.bfloat16)
    upd_key = jnp.einsum(
        "rmc,rck->rmk",
        shrink[:, :, rank_portion : 2 * rank_portion],
        own_kv[:, 0],
        preferred_element_type=jnp.float32,
    ).astype(jnp.bfloat16)
    upd_value = jnp.einsum(
        "rmc,rck->rmk",
        shrink[:, :, 2 * rank_portion :],
        own_kv[:, 1],
        preferred_element_type=jnp.float32,
    ).astype(jnp.bfloat16)
    upd_kv = jnp.stack([upd_key, upd_value], axis=2)
    back_query = lax.all_to_all(upd_query[None], "replica", split_axis=1, concat_axis=0, tiled=True)
    back_kv = lax.all_to_all(upd_kv[None], "replica", split_axis=1, concat_axis=0, tiled=True)
    query_correction = jnp.einsum(
        "sg,gmk->smk", picker, back_query[:, 0], preferred_element_type=jnp.float32
    ).astype(jnp.bfloat16)
    both_deltas = jnp.einsum(
        "sg,gmtk->smtk", picker, back_kv[:, 0], preferred_element_type=jnp.float32
    ).astype(jnp.bfloat16)
    key_correction = both_deltas[:, :, 0]
    value_correction = both_deltas[:, :, 1]
    query_rows = (
        rotated_base_query.astype(jnp.float32)
        + ADAPTER_SCALE
        * query_correction.reshape(request_list, token_rows, query_column_span).astype(jnp.float32)
    ).astype(jnp.bfloat16)
    base_quartet = base_kv.reshape(request_list, token_rows, 2, head_column_span)
    incoming_keys = (
        base_quartet[:, :, 0]
        + ADAPTER_SCALE
        * key_correction.reshape(request_list, token_rows, head_column_span).astype(jnp.float32)
    ).astype(jnp.bfloat16)
    incoming_values = (
        base_quartet[:, :, 1]
        + ADAPTER_SCALE
        * value_correction.reshape(request_list, token_rows, head_column_span).astype(jnp.float32)
    ).astype(jnp.bfloat16)
    kv_heads = head_column_span // HEAD_WIDTH
    group_size = query_column_span // HEAD_WIDTH // kv_heads
    inv_root = 1.0 / math.sqrt(HEAD_WIDTH)
    query_heads = query_rows.reshape(request_list, token_rows, kv_heads, group_size, HEAD_WIDTH)
    cache_keys = key_value_cache[:, 0].reshape(request_list, CTX, kv_heads, HEAD_WIDTH)
    cache_values = key_value_cache[:, 1].reshape(request_list, CTX, kv_heads, HEAD_WIDTH)
    fresh_keys = incoming_keys.reshape(request_list, token_rows, kv_heads, HEAD_WIDTH)
    fresh_values = incoming_values.reshape(request_list, token_rows, kv_heads, HEAD_WIDTH)
    past_scores = (
        jnp.einsum("rpkgd,rjkd->rkgpj", query_heads, cache_keys, preferred_element_type=jnp.float32)
        * inv_root
    )
    fresh_scores = (
        jnp.einsum("rpkgd,rjkd->rkgpj", query_heads, fresh_keys, preferred_element_type=jnp.float32)
        * inv_root
    )
    scores = jnp.concatenate([past_scores, fresh_scores], axis=4)
    key_spots = jnp.arange(CTX + token_rows, dtype=jnp.int32)
    cached_ok = key_spots[None, :] < cache_length[:, None]
    fresh_ok = key_spots[None, :] - CTX <= jnp.arange(token_rows, dtype=jnp.int32)[:, None]
    allowed = jnp.where(key_spots[None, None, :] >= CTX, fresh_ok[None], cached_ok[:, None, :])
    scores = jnp.where(allowed[:, None, None], scores, -jnp.inf)
    row_top = jnp.max(scores, axis=4, keepdims=True)
    lifted = jnp.exp(scores - row_top)
    weights = (lifted / jnp.sum(lifted, axis=4, keepdims=True)).astype(jnp.bfloat16)
    attended = jnp.einsum(
        "rkgpj,rjkd->rpkgd", weights[..., :CTX], cache_values, preferred_element_type=jnp.float32
    )
    attended = attended + jnp.einsum(
        "rkgpj,rjkd->rpkgd", weights[..., CTX:], fresh_values, preferred_element_type=jnp.float32
    )
    seg_slot = jnp.arange(request_list, dtype=jnp.int32) % seg_size
    live_rows = seg_slot < jnp.repeat(segment_live_requests, seg_size)
    attended = jnp.where(live_rows[:, None, None, None, None], attended, 0.0)
    return attended.reshape(request_list, token_rows, query_column_span).astype(jnp.bfloat16)


def solution(mesh):
    return jax.shard_map(
        shards,
        mesh=mesh,
        in_specs=(
            P("replica", None, "tensor"),
            P("replica", None, "tensor"),
            P(None, None, "tensor"),
            P("replica", None, None, "tensor"),
            P("replica", None, "tensor"),
            P("replica", None, "tensor"),
            P("replica", None, None, "tensor"),
            P(),
            P(),
            P("replica"),
            P("replica"),
        ),
        out_specs=P("replica", None, "tensor"),
        check_vma=False,
    )
```

profile of v0, /device:TPU:1, one launch (start us, length us, event | category | flops | bytes accessed | tf_op | source)
XLA Modules:
  0.0 233.7 jit_solution(13105066959938305469)
XLA Ops:
  6.5 2.7 %copy.85 = bf16[256,2,1024]{2,0,1:T(8,128)(2,1)} copy(bf16[256,2,1024]{2,1,0:T(2,128)(2,1)} %param.11) | data formatting | bytes 2097152 | tf_op args[0]
  11.0 2.2 convert_bitcast_fusion.1
  13.2 2.5 %copy.76 = bf16[32,1,32,1024]{3,2,1,0:T(8,128)(2,1)} copy(bf16[32,1,32,1024]{3,0,2,1:T(8,128)(2,1)S(1)} %convert_bitcast_fusion.1) | data formatting | bytes 4194304 | tf_op jit(solution)/shard_map/broadcast_in_dim | solution.py:75
  15.7 8.8 %all-to-all-start = ((bf16[32,1,32,1024]{3,2,1,0:T(8,128)(2,1)}), bf16[32,1,32,1024]{3,2,1,0:T(8,128)(2,1)}, u32[]{:S(2)}, u32[]{:S(2)}) async-start(bf16[32,1,32,1024]{3,2,1,0:T(8,128)(2,1)} %copy.76), calls=%async_computation | async-start | bytes 4194304 | tf_op jit(solution)/shard_map/all_to_all | solution.py:80
  25.2 6.6 %convolution_convert_fusion = bf16[32,192,1024]{2,0,1:T(8,128)(2,1)} fusion(bf16[4,192,1024]{2,1,0:T(8,128)(2,1)S(1)} %copy-done, s32[32]{0:T(128)S(1)} %fusion.48, pred[32]{0:T(512)(128)(4,1)S(1)} %get-tuple-element.7), kind=kOutput, calls=%fused_computation.4 | convolution fusion | flops 56623360 | bytes 14155936 | tf_op jit(solution)/shard_map/nu,uwt->nwt/dot_general | solution.py:65
  31.8 20.5 %all-to-all-done = bf16[32,1,32,1024]{3,2,1,0:T(8,128)(2,1)} async-done(((bf16[32,1,32,1024]{3,2,1,0:T(8,128)(2,1)}), bf16[32,1,32,1024]{3,2,1,0:T(8,128)(2,1)}, u32[]{:S(2)}, u32[]{:S(2)}) %all-to-all-start) | async-done | bytes 2097184 | tf_op jit(solution)/shard_map/all_to_all | solution.py:80
  52.3 12.2 %fusion = f32[32,32,192]{2,1,0:T(8,128)S(1)} fusion(bf16[32,192,1024]{2,0,1:T(8,128)(2,1)} %convolution_convert_fusion, bf16[32,1,32,1024]{3,2,1,0:T(8,128)(2,1)} %all-to-all-done), kind=kOutput, calls=%fused_computation | convolution fusion | flops 402653184 | bytes 15466496 | tf_op jit(solution)/shard_map/rmd,rcd->rmc/dot_general | solution.py:78
  64.5 68.8 %all-reduce.1 = bf16[32,32,192]{2,1,0:T(8,128)(2,1)S(1)} all-reduce(f32[32,32,192]{2,1,0:T(8,128)S(1)} %fusion), channel_id=1, replica_groups=mesh['replica'=32,'tensor'=8] {'tensor'}, use_global_device_ids=true, to_apply=%region_3.4 | all-reduce | flops 196608 | bytes 1179648 | tf_op jit(solution)/shard_map/psum | solution.py:84
  134.8 13.9 %all-to-all-start.2 = ((bf16[1,32,32,2,128]{4,2,3,0,1:T(8,128)(2,1)}), bf16[1,32,32,2,128]{4,2,3,0,1:T(8,128)(2,1)S(1)}, u32[]{:S(2)}, u32[]{:S(2)}) async-start(bf16[1,32,32,2,128]{4,2,3,0,1:T(8,128)(2,1)} %copy.90), calls=%async_computation.2 | async-start | bytes 1048576 | tf_op jit(solution)/shard_map/all_to_all | solution.py:102
  150.1 6.5 %convert_bitcast_fusion = bf16[1,32,32,1024]{3,2,0,1:T(8,128)(2,1)} fusion(bf16[32,64,1024]{2,0,1:T(8,128)(2,1)S(1)} %convolution_convert_fusion.1, bf16[32,32,192]{2,1,0:T(8,128)(2,1)S(1)} %all-reduce.1), kind=kOutput, calls=%fused_computation.29 | convolution fusion | flops 135266304 | bytes 6553600 | tf_op jit(solution)/shard_map/rmc,rck->rmk/dot_general | solution.py:85
  156.5 3.9 %all-to-all-done.2 = bf16[1,32,32,2,128]{4,2,3,0,1:T(8,128)(2,1)S(1)} async-done(((bf16[1,32,32,2,128]{4,2,3,0,1:T(8,128)(2,1)}), bf16[1,32,32,2,128]{4,2,3,0,1:T(8,128)(2,1)S(1)}, u32[]{:S(2)}, u32[]{:S(2)}) %all-to-all-start.2) | async-done | bytes 524320 | tf_op jit(solution)/shard_map/all_to_all | solution.py:102
  160.4 4.8 %all-to-all-start.1 = ((bf16[1,32,32,1024]{3,2,0,1:T(8,128)(2,1)}), bf16[1,32,32,1024]{3,2,0,1:T(8,128)(2,1)}, u32[]{:S(2)}, u32[]{:S(2)}) async-start(bf16[1,32,32,1024]{3,2,0,1:T(8,128)(2,1)} %convert_bitcast_fusion), calls=%async_computation.1 | async-start | bytes 4194304 | tf_op jit(solution)/shard_map/all_to_all | solution.py:101
  165.2 4.7 %copy.158 = bf16[1024,8,2,128]{3,1,2,0:T(8,128)(2,1)} copy(bf16[1024,8,2,128]{3,2,1,0:T(2,128)(2,1)} %bitcast.131) | data formatting | bytes 8388608
  169.9 6.4 %copy.86 = bf16[256,8192]{1,0:T(8,128)(2,1)} copy(bf16[256,8192]{0,1:T(8,128)(2,1)} %bitcast.130) | data formatting | bytes 8388608 | tf_op jit(solution)/shard_map/dot_general | solution.py:41
  177.5 15.5 %all-to-all-done.1 = bf16[1,32,32,1024]{3,2,0,1:T(8,128)(2,1)} async-done(((bf16[1,32,32,1024]{3,2,0,1:T(8,128)(2,1)}), bf16[1,32,32,1024]{3,2,0,1:T(8,128)(2,1)}, u32[]{:S(2)}, u32[]{:S(2)}) %all-to-all-start.1) | async-done | bytes 2097184 | tf_op jit(solution)/shard_map/all_to_all | solution.py:101
  193.0 4.0 %convert_multiply_fusion = f32[16,32,1024]{2,0,1:T(8,128)S(1)} fusion(bf16[1,32,32,1024]{3,2,0,1:T(8,128)(2,1)} %all-to-all-done.1, s32[16]{0:T(128)S(1)} %dynamic-slice_bitcast_fusion), kind=kOutput, calls=%fused_computation.28 | convolution fusion | flops 35127808 | bytes 4194368 | tf_op jit(solution)/shard_map/sg,gmk->smk/dot_general | solution.py:103
  197.0 2.5 %copy.83 = f32[16,32,1024]{2,1,0:T(8,128)} copy(f32[16,32,1024]{2,0,1:T(8,128)S(1)} %convert_multiply_fusion) | data formatting | bytes 4194304 | tf_op jit(solution)/shard_map/mul | solution.py:113
  199.5 3.6 %mul.64 = f32[256,2,1024]{2,1,0:T(2,128)} reshape(f32[16,32,1024]{2,1,0:T(8,128)} %copy.83) | data formatting | bytes 4194304 | tf_op jit(solution)/shard_map/mul | solution.py:113
  203.1 2.7 %add_convert_fusion = bf16[256,2,1024]{2,1,0:T(2,128)(2,1)S(1)} fusion(f32[256,2,1024]{2,1,0:T(2,128)} %mul.64, bf16[256,2,1024]{2,1,0:T(2,128)(2,1)S(1)} %copy-done.5), kind=kLoop, calls=%fused_computation.27 | loop fusion | flops 1572864 | bytes 4194304 | tf_op jit(solution)/shard_map/convert_element_type | solution.py:115
  206.5 4.1 %multiply_bitcast_fusion.1 = f32[256,1,8,2,32]{4,2,3,0,1:T(8,128)} fusion(bf16[256,2,8,128]{3,2,1,0:T(8,128)(2,1)S(1)} %reshape.268, bf16[256,2,32,128]{3,2,1,0:T(8,128)(2,1)} %param.14), kind=kOutput, calls=%fused_computation.25 | convolution fusion | flops 33685504 | bytes 3670016 | tf_op jit(solution)/shard_map/rpkgd,rjkd->rkgpj/dot_general | solution.py:136
  210.7 6.1 %fusion.2 = f32[256,2,2,128]{3,0,2,1:T(8,128)S(1)} fusion(bf16[2,128,8192,1]{2,1,0,3:T(8,128)(2,1)} %bitcast.132, bf16[256,2,8192]{2,0,1:T(8,128)(2,1)} %all-gather.2.cloned.1.call-done), kind=kOutput, calls=%fused_computation.2 | convolution fusion | flops 2147483648 | bytes 13107200 | tf_op jit(solution)/shard_map/dot_general | solution.py:41
  218.3 1.5 fusion.67
  219.8 1.7 fusion.19
  223.7 2.1 fusion.28
  (58 shorter events, 11.8 us)
Async XLA Ops:
  6.5 18.7 %copy-start = (bf16[4,192,1024]{2,1,0:T(8,128)(2,1)S(1)}, bf16[4,192,1024]{2,1,0:T(8,128)(2,1)}, u32[]{:S(2)}) copy-start(bf16[4,192,1024]{2,1,0:T(8,128)(2,1)} %param.15) | copy-start | bytes 4718596
  6.5 2.7 %copy-start.4 = (bf16[256,2,1024]{2,1,0:T(2,128)(2,1)S(1)}, bf16[256,2,1024]{2,1,0:T(2,128)(2,1)}, u32[]{:S(2)}) copy-start(bf16[256,2,1024]{2,1,0:T(2,128)(2,1)} %param.11) | copy-start | bytes 3145732
  6.5 204.1 %all-gather.2.cloned.1.call-start = ((), (), s32[]{:S(2)}) async-start(), calls=%async_computation.3 | async-start | bytes 9437184 | tf_op jit(solution)/shard_map/all_gather | solution.py:39
  9.2 1.3 copy-start.8
  9.3 1.3 copy-start.10
  15.7 8.9 %copy-start.7 = (bf16[4,2,64,128]{3,2,1,0:T(8,128)(2,1)S(1)}, bf16[4,2,64,128]{3,2,1,0:T(8,128)(2,1)}, u32[]{:S(2)}) copy-start(bf16[4,2,64,128]{3,2,1,0:T(8,128)(2,1)} %param.17) | copy-start | bytes 393220
  15.7 36.6 %all-to-all-start = ((bf16[32,1,32,1024]{3,2,1,0:T(8,128)(2,1)}), bf16[32,1,32,1024]{3,2,1,0:T(8,128)(2,1)}, u32[]{:S(2)}, u32[]{:S(2)}) async-start(bf16[32,1,32,1024]{3,2,1,0:T(8,128)(2,1)} %copy.76), calls=%async_computation | async-start | bytes 4194304 | tf_op jit(solution)/shard_map/all_to_all | solution.py:80
  133.6 15.2 %copy-start.6 = (bf16[4,64,1024]{2,1,0:T(8,128)(2,1)S(1)}, bf16[4,64,1024]{2,1,0:T(8,128)(2,1)}, u32[]{:S(2)}) copy-start(bf16[4,64,1024]{2,1,0:T(8,128)(2,1)} %param.16) | copy-start | bytes 1572868
  134.8 25.6 %all-to-all-start.2 = ((bf16[1,32,32,2,128]{4,2,3,0,1:T(8,128)(2,1)}), bf16[1,32,32,2,128]{4,2,3,0,1:T(8,128)(2,1)S(1)}, u32[]{:S(2)}, u32[]{:S(2)}) async-start(bf16[1,32,32,2,128]{4,2,3,0,1:T(8,128)(2,1)} %copy.90), calls=%async_computation.2 | async-start | bytes 1048576 | tf_op jit(solution)/shard_map/all_to_all | solution.py:102
  160.4 32.6 %all-to-all-start.1 = ((bf16[1,32,32,1024]{3,2,0,1:T(8,128)(2,1)}), bf16[1,32,32,1024]{3,2,0,1:T(8,128)(2,1)}, u32[]{:S(2)}, u32[]{:S(2)}) async-start(bf16[1,32,32,1024]{3,2,0,1:T(8,128)(2,1)} %convert_bitcast_fusion), calls=%async_computation.1 | async-start | bytes 4194304 | tf_op jit(solution)/shard_map/all_to_all | solution.py:101
  169.9 6.4 %copy-start.11 = (s32[16]{0:T(128)S(1)}, s32[16]{0:T(128)}, u32[]{:S(2)}) copy-start(s32[16]{0:T(128)} %param.20) | copy-start | bytes 196
  169.9 6.6 %copy-start.9 = (s32[256]{0:T(256)S(1)}, s32[256]{0:T(256)}, u32[]{:S(2)}) copy-start(s32[256]{0:T(256)} %param.21) | copy-start | bytes 3076
  199.5 3.6 %copy-start.5 = (bf16[256,2,1024]{2,1,0:T(2,128)(2,1)S(1)}, bf16[256,2,1024]{2,1,0:T(2,128)(2,1)}, u32[]{:S(2)}) copy-start(bf16[256,2,1024]{2,1,0:T(2,128)(2,1)} %param.12) | copy-start | bytes 3145732
  216.7 1.6 copy-start.2
  219.8 3.2 %copy-start.3 = (bf16[256,2,32,128]{3,2,1,0:T(8,128)(2,1)S(1)}, bf16[256,2,32,128]{3,2,1,0:T(8,128)(2,1)}, u32[]{:S(2)}) copy-start(bf16[256,2,32,128]{3,2,1,0:T(8,128)(2,1)} %param.14) | copy-start | bytes 12582916
  223.6 3.2 %copy-start.1 = (bf16[4,192,1024]{2,1,0:T(8,128)(2,1)S(1)}, bf16[4,192,1024]{2,1,0:T(8,128)(2,1)}, u32[]{:S(2)}) copy-start(bf16[4,192,1024]{2,1,0:T(8,128)(2,1)} %param.15) | copy-start | bytes 4718596
Sparse Core Ops, SparseCore 0:
  9.4 109.6 all-gather.1
where the time goes:
time: 234 us
  blocking collectives  68.8 us (29%)
  matrix products  47.6 us (20%)
  waiting for transfers between devices  39.9 us (17%)
  local copies, waits for them, and re-layouts  28 us (12%)
  starting transfers between devices  27.5 us (12%)
  between operations  13.7 us (6%)
  other arithmetic  8.24 us (4%)
    psum x1, blocking collectives, shards(): shrink = lax.psum(partial_value, 'tensor').astype(jnp.bfloat16)  68.8 us
    all_to_all x1, waiting for transfers between devices, shards(): lax.all_to_all(outgoing, 'replica', split_axis=0, concat_axis=1, tiled=True)  20.5 us
    all_to_all x1, waiting for transfers between devices, shards(): lax.all_to_all(upd_query[None], 'replica', split_axis=1, concat_axis=0, t...  15.5 us
    all_to_all x1, starting transfers between devices, shards(): lax.all_to_all(upd_kv[None], 'replica', split_axis=1, concat_axis=0, tile...  13.9 us
    dot_general x1, matrix products, shards(): jnp.einsum('rmd,rcd->rmc', lax.all_to_all(outgoing, 'replica', split_axis...  12.2 us
    all_to_all x1, starting transfers between devices, shards(): lax.all_to_all(outgoing, 'replica', split_axis=0, concat_axis=1, tiled=True)  8.79 us
    unnamed x26, local copies, waits for them, and re-layouts  8.53 us
    dot_general x1, matrix products, shards(): jnp.einsum('nu,uwt->nwt', offered_rows, adapter_down_maps, preferred_elem...  6.58 us
  transfers between devices with their start and end apart: 4, of which 3 were waited for; matrix products, arithmetic and copies ran while one was open for 28% of the time, Pallas kernels for 0%

commit v1 on v0

v1 whole, which is shorter than its diff:
```python
import functools
import math

import jax
import jax.numpy as jnp
from jax import lax
from jax.experimental import pallas as pl
from jax.experimental.pallas import tpu as pltpu
from jax.sharding import PartitionSpec as P

HEAD_WIDTH = 128
CTX = 32
ADAPTER_SCALE = 0.5
MESH = pl.DeviceIdType.MESH

RINGS = (
    ((2, 2),),
    ((2, 1), (1, 2), (2, 3), (3, 2)),
    ((0, 2), (2, 0)),
    ((1, 1), (3, 3), (1, 3), (3, 1)),
    ((0, 1), (1, 0), (0, 3), (3, 0)),
)
OFFSETS = [(0, 0, 0)] + [(dy, dx, dc) for ring in RINGS for dc in (0, 1) for dy, dx in ring] + [(0, 0, 1)]
SLOTS = 32
CHUNKS = 4
PER = SLOTS // CHUNKS
TZ = 8


def packed(chunk, which, bits):
    total = 0
    for j in range(PER):
        total += OFFSETS[chunk * PER + j][which] << (bits * j)
    return total


PACK_Y = [packed(c, 0, 2) for c in range(CHUNKS)]
PACK_X = [packed(c, 1, 2) for c in range(CHUNKS)]
PACK_C = [packed(c, 2, 1) for c in range(CHUNKS)]


def offset(chunk, j):
    return (
        (PACK_Y[chunk] >> (2 * j)) & 3,
        (PACK_X[chunk] >> (2 * j)) & 3,
        (PACK_C[chunk] >> j) & 1,
    )


def moved(me, off, sign):
    y, x, c = me // 8, (me // 2) % 4, me % 2
    dy, dx, dc = off
    return ((y + 4 + sign * dy) % 4) * 8 + ((x + 4 + sign * dx) % 4) * 2 + (c + dc) % 2


def exchange_kernel(
    seg_of_group, group_of_seg, local_of_replica, x_ref, down_ref, upq_ref, upkv_ref, out_ref,
    xs, xr, part, rs, ag, ds, dr,
    x_send, x_recv, rs_send, rs_recv, ag_send, ag_recv, d_send, d_recv,
):
    me = lax.axis_index("replica")
    t = lax.axis_index("tensor")

    barrier = pltpu.get_barrier_semaphore()

    def greet_plane(i, _):
        pl.semaphore_signal(barrier, inc=1, device_id=((me + i) % SLOTS, t), device_id_type=MESH)
        return 0

    def greet_z(i, _):
        pl.semaphore_signal(barrier, inc=1, device_id=(me, (t + i) % TZ), device_id_type=MESH)
        return 0

    lax.fori_loop(1, SLOTS, greet_plane, 0)
    lax.fori_loop(1, TZ, greet_z, 0)

    def x_copy(chunk, j):
        p = chunk * PER + j
        return pltpu.make_async_remote_copy(
            src_ref=xs.at[p], dst_ref=xr.at[p], send_sem=x_send.at[p], recv_sem=x_recv.at[p],
            device_id=(moved(me, offset(chunk, j), 1), t), device_id_type=MESH,
        )

    def d_copy(chunk, j):
        p = chunk * PER + j
        return pltpu.make_async_remote_copy(
            src_ref=ds.at[p], dst_ref=dr.at[me], send_sem=d_send.at[p], recv_sem=d_recv.at[p],
            device_id=(moved(me, offset(chunk, j), -1), t), device_id_type=MESH,
        )

    def rs_copy(chunk, u, sender):
        return pltpu.make_async_remote_copy(
            src_ref=part.at[chunk * PER + u], dst_ref=rs.at[chunk, sender],
            send_sem=rs_send.at[chunk, u], recv_sem=rs_recv.at[chunk, sender],
            device_id=(me, u), device_id_type=MESH,
        )

    def ag_copy(chunk, u, sender):
        return pltpu.make_async_remote_copy(
            src_ref=ag.at[chunk, sender], dst_ref=ag.at[chunk, sender],
            send_sem=ag_send.at[chunk, u], recv_sem=ag_recv.at[chunk, sender],
            device_id=(me, u), device_id_type=MESH,
        )

    for chunk in range(CHUNKS):
        def fill(j, _, chunk=chunk):
            group = moved(me, offset(chunk, j), 1)
            xs[chunk * PER + j] = x_ref[seg_of_group[group]]
            return 0

        lax.fori_loop(0, PER, fill, 0)
    pl.semaphore_wait(barrier, SLOTS - 1 + TZ - 1)
    for chunk in range(CHUNKS):
        def send(j, _, chunk=chunk):
            x_copy(chunk, j).start()
            return 0

        lax.fori_loop(1 if chunk == 0 else 0, PER, send, 0)

    def shrink_parts(chunk):
        def one(j, _):
            p = chunk * PER + j
            rows = xs[0] if chunk == 0 and isinstance(j, int) else xr[p]
            w = down_ref[local_of_replica[moved(me, offset(chunk, j), -1)]]
            part[p] = lax.dot_general(
                rows, w, (((1,), (1,)), ((), ())), preferred_element_type=jnp.float32
            ).astype(jnp.bfloat16)
            return 0

        def arrived(j, _):
            x_copy(chunk, j).wait_recv()
            return one(j, 0)

        if chunk == 0:
            one(0, 0)
        lax.fori_loop(1 if chunk == 0 else 0, PER, arrived, 0)

        def send(i, _):
            rs_copy(chunk, (t + i) % TZ, t).start()
            return 0

        lax.fori_loop(1, TZ, send, 0)

    def add_up(chunk):
        def wait(i, _):
            rs_copy(chunk, t, (t + TZ - i) % TZ).wait_recv()
            return 0

        lax.fori_loop(1, TZ, wait, 0)
        rs[chunk, t] = part[chunk * PER + t]
        total = rs[chunk, 0].astype(jnp.float32)
        for u in range(1, TZ):
            total = total + rs[chunk, u].astype(jnp.float32)
        ag[chunk, t] = total.astype(jnp.bfloat16)

        def send(i, _):
            ag_copy(chunk, (t + i) % TZ, t).start()
            return 0

        lax.fori_loop(1, TZ, send, 0)

    def give_back(chunk):
        def wait(i, _):
            ag_copy(chunk, t, (t + TZ - i) % TZ).wait_recv()
            return 0

        lax.fori_loop(1, TZ, wait, 0)

        def deltas(j):
            a = local_of_replica[moved(me, offset(chunk, j), -1)]
            shrink = ag[chunk, j]
            q = jnp.dot(shrink[:, 0:64], upq_ref[a], preferred_element_type=jnp.float32)
            k = jnp.dot(shrink[:, 64:128], upkv_ref[a, 0], preferred_element_type=jnp.float32)
            v = jnp.dot(shrink[:, 128:192], upkv_ref[a, 1], preferred_element_type=jnp.float32)
            return jnp.concatenate([q, k, v], axis=1).astype(jnp.bfloat16)

        def one(j, _):
            ds[chunk * PER + j] = deltas(j)
            d_copy(chunk, j).start()
            return 0

        if chunk == 0:
            dr[me] = deltas(0)
        lax.fori_loop(1 if chunk == 0 else 0, PER, one, 0)

    shrink_parts(0)
    shrink_parts(1)
    add_up(0)
    shrink_parts(2)
    add_up(1)
    give_back(0)
    shrink_parts(3)
    add_up(2)
    give_back(1)
    add_up(3)
    give_back(2)
    give_back(3)

    for chunk in range(CHUNKS):
        def settle(j, _, chunk=chunk):
            d_copy(chunk, j).wait_recv()
            return 0

        lax.fori_loop(1 if chunk == 0 else 0, PER, settle, 0)

    def gather(s, _):
        out_ref[s] = dr[group_of_seg[s]]
        return 0

    lax.fori_loop(0, out_ref.shape[0], gather, 0)

    for chunk in range(CHUNKS):
        def settle(j, _, chunk=chunk):
            x_copy(chunk, j).wait_send()
            d_copy(chunk, j).wait_send()
            return 0

        lax.fori_loop(1 if chunk == 0 else 0, PER, settle, 0)

        def settle_z(i, _, chunk=chunk):
            rs_copy(chunk, (t + i) % TZ, t).wait_send()
            ag_copy(chunk, (t + i) % TZ, t).wait_send()
            return 0

        lax.fori_loop(1, TZ, settle_z, 0)


def exchange(seg_of_group, group_of_seg, local_of_replica, x, down, upq, upkv):
    segs, rows, features = x.shape
    ranks = down.shape[1]
    columns = upq.shape[2] + 2 * upkv.shape[3]
    smem = pl.BlockSpec(memory_space=pltpu.SMEM)
    vmem = pl.BlockSpec(memory_space=pltpu.VMEM)
    dma = pltpu.SemaphoreType.DMA
    return pl.pallas_call(
        exchange_kernel,
        out_shape=jax.ShapeDtypeStruct((segs, rows, columns), jnp.bfloat16),
        in_specs=[smem] * 3 + [vmem] * 4,
        out_specs=vmem,
        scratch_shapes=[
            pltpu.VMEM((SLOTS, rows, features), jnp.bfloat16),
            pltpu.VMEM((SLOTS, rows, features), jnp.bfloat16),
            pltpu.VMEM((SLOTS, rows, ranks), jnp.bfloat16),
            pltpu.VMEM((CHUNKS, TZ, rows, ranks), jnp.bfloat16),
            pltpu.VMEM((CHUNKS, TZ, rows, ranks), jnp.bfloat16),
            pltpu.VMEM((SLOTS, rows, columns), jnp.bfloat16),
            pltpu.VMEM((SLOTS, rows, columns), jnp.bfloat16),
            dma((SLOTS,)), dma((SLOTS,)),
            dma((CHUNKS, TZ)), dma((CHUNKS, TZ)), dma((CHUNKS, TZ)), dma((CHUNKS, TZ)),
            dma((SLOTS,)), dma((SLOTS,)),
        ],
        compiler_params=pltpu.CompilerParams(
            collective_id=0, has_side_effects=True, vmem_limit_bytes=40 * 2**20
        ),
        cost_estimate=pl.CostEstimate(flops=10**9, bytes_accessed=200 * 2**20, transcendentals=0),
        name="exchange",
    )(seg_of_group, group_of_seg, local_of_replica, x, down, upq, upkv)


def attend_kernel(live, q_ref, delta_ref, base_ref, cache_ref, bias_ref, out_ref):
    s = pl.program_id(0)
    heads = q_ref.shape[1] // HEAD_WIDTH
    wide = q_ref.shape[1]
    half = 8
    delta = delta_ref[0].astype(jnp.float32) * ADAPTER_SCALE
    q_all = (q_ref[...].astype(jnp.float32) + delta[:, :wide]).astype(jnp.bfloat16)
    fresh = (base_ref[...] + delta[:, wide:]).astype(jnp.bfloat16)
    rows = half * 2
    n = heads * rows
    row = lax.broadcasted_iota(jnp.int32, (n, half * CTX), 0)
    col = lax.broadcasted_iota(jnp.int32, (n, half * CTX), 1)
    same = (row % rows) // 2 == col // CTX
    row = lax.broadcasted_iota(jnp.int32, (n, rows), 0) % rows
    col = lax.broadcasted_iota(jnp.int32, (n, rows), 1)
    same_fresh = (row // 2 == col // 2) & (col <= row)
    scale = 1.0 / math.sqrt(HEAD_WIDTH)
    for h in range(2):
        at = slice(h * rows, (h + 1) * rows)
        q = jnp.concatenate(
            [q_all[at, g * HEAD_WIDTH : (g + 1) * HEAD_WIDTH] for g in range(heads)], axis=0
        )
        keys = cache_ref[h * half : (h + 1) * half, 0].reshape(half * CTX, HEAD_WIDTH)
        values = cache_ref[h * half : (h + 1) * half, 1].reshape(half * CTX, HEAD_WIDTH)
        new_keys = fresh[at, :HEAD_WIDTH]
        new_values = fresh[at, HEAD_WIDTH:]
        nt = (((1,), (1,)), ((), ()))
        old = lax.dot_general(q, keys, nt, preferred_element_type=jnp.float32) * scale
        new = lax.dot_general(q, new_keys, nt, preferred_element_type=jnp.float32) * scale
        old = jnp.where(same, old + bias_ref[0, h : h + 1], -jnp.inf)
        new = jnp.where(same_fresh, new, -jnp.inf)
        top = jnp.maximum(
            jnp.max(old, axis=1, keepdims=True), jnp.max(new, axis=1, keepdims=True)
        )
        old = jnp.exp(old - top)
        new = jnp.exp(new - top)
        total = jnp.sum(old, axis=1, keepdims=True) + jnp.sum(new, axis=1, keepdims=True)
        mixed = jnp.dot(old.astype(jnp.bfloat16), values, preferred_element_type=jnp.float32)
        mixed = mixed + jnp.dot(
            new.astype(jnp.bfloat16), new_values, preferred_element_type=jnp.float32
        )
        mixed = mixed / total
        out = jnp.concatenate([mixed[g * rows : (g + 1) * rows] for g in range(heads)], axis=1)
        place = h * half + lax.broadcasted_iota(jnp.int32, out.shape, 0) // 2
        out_ref[at, :] = jnp.where(place < live[s], out, 0.0).astype(jnp.bfloat16)


def attend(live, q, delta, base, cache, bias):
    segs = live.shape[0]
    rows, wide = q.shape
    per = rows // segs
    return pl.pallas_call(
        attend_kernel,
        grid_spec=pltpu.PrefetchScalarGridSpec(
            num_scalar_prefetch=1,
            grid=(segs,),
            in_specs=[
                pl.BlockSpec((per, wide), lambda s, _: (s, 0)),
                pl.BlockSpec((1,) + delta.shape[1:], lambda s, _: (s, 0, 0)),
                pl.BlockSpec((per, base.shape[1]), lambda s, _: (s, 0)),
                pl.BlockSpec((cache.shape[0] // segs,) + cache.shape[1:], lambda s, _: (s, 0, 0, 0)),
                pl.BlockSpec((1,) + bias.shape[1:], lambda s, _: (s, 0, 0)),
            ],
            out_specs=pl.BlockSpec((per, wide), lambda s, _: (s, 0)),
        ),
        out_shape=jax.ShapeDtypeStruct((rows, wide), jnp.bfloat16),
        compiler_params=pltpu.CompilerParams(vmem_limit_bytes=24 * 2**20),
        name="attend",
    )(live, q, delta, base, cache, bias)


def shards(
    normed_token_input,
    rotated_base_query,
    key_value_weight,
    key_value_cache,
    adapter_down_maps,
    query_up_maps,
    key_value_up_maps,
    adapter_storage_row,
    segment_adapter,
    segment_live_requests,
    cache_length,
):
    requests, tokens, features = normed_token_input.shape
    wide = rotated_base_query.shape[2]
    kv_wide = key_value_weight.shape[2]
    owned = adapter_down_maps.shape[0]
    replicas = lax.axis_size("replica")
    segs = segment_live_requests.shape[0]
    me = lax.axis_index("replica")

    adapter_ids = jnp.arange(adapter_storage_row.shape[0], dtype=jnp.int32)
    slot = jnp.sum(
        jnp.where(
            segment_adapter[:, None] == adapter_ids[None, :], adapter_storage_row[None, :], 0
        ),
        axis=1,
    ).reshape(replicas, segs)
    group, local = slot // owned, slot % owned
    group_of_seg = lax.dynamic_index_in_dim(group, me, 0, keepdims=False)
    group_ids = jnp.arange(replicas, dtype=jnp.int32)
    seg_ids = jnp.arange(segs, dtype=jnp.int32)
    seg_of_group = jnp.sum(
        jnp.where(group_of_seg[None, :] == group_ids[:, None], seg_ids[None, :], 0), axis=1
    )
    local_of_replica = jnp.sum(jnp.where(group == me, local, 0), axis=1)

    gathered = lax.all_gather(normed_token_input, "tensor", axis=2, tiled=True)
    base_kv = jnp.dot(
        gathered.reshape(-1, gathered.shape[2]),
        key_value_weight.reshape(-1, 2 * kv_wide),
        preferred_element_type=jnp.float32,
    )
    delta = exchange(
        seg_of_group, group_of_seg, local_of_replica,
        normed_token_input.reshape(segs, requests * tokens // segs, features),
        adapter_down_maps, query_up_maps, key_value_up_maps,
    )
    spots = jnp.arange(CTX, dtype=jnp.int32)
    bias = jnp.where(spots[None, :] < cache_length[:, None], 0.0, -jnp.inf).astype(jnp.float32)
    out = attend(
        segment_live_requests, rotated_base_query.reshape(requests * tokens, wide), delta, base_kv,
        key_value_cache, bias.reshape(segs, 2, requests // segs // 2 * CTX),
    )
    return out.reshape(requests, tokens, wide)


def solution(mesh):
    return jax.shard_map(
        shards,
        mesh=mesh,
        in_specs=(
            P("replica", None, "tensor"),
            P("replica", None, "tensor"),
            P(None, None, "tensor"),
            P("replica", None, None, "tensor"),
            P("replica", None, "tensor"),
            P("replica", None, "tensor"),
            P("replica", None, None, "tensor"),
            P(),
            P(),
            P("replica"),
            P("replica"),
        ),
        out_specs=P("replica", None, "tensor"),
        check_vma=False,
    )
```

time: 234 us -> 179 us (0.76)
  the two profiles are of different devices: /device:TPU:1 before, /device:TPU:2 now
where the time goes in v1:
time: 179 us; the launch traced here: 178 us
  Pallas kernels  89.5 us (50%)
  waiting for transfers between devices  46.3 us (26%)
  local copies, waits for them, and re-layouts  20.4 us (11%)
  between operations  13.5 us (8%)
  matrix products  7.06 us (4%)
    pallas_call x1, Pallas kernels, exchange(): pl.pallas_call(exchange_kernel, out_shape=jax.ShapeDtypeStruct((segs, row...  77.7 us
    all_gather x1, waiting for transfers between devices, shards(): gathered = lax.all_gather(normed_token_input, 'tensor', axis=2, tiled=True)  45.6 us
    reshape x1, local copies, waits for them, and re-layouts, shards(): gathered.reshape(-1, gathered.shape[2])  13.1 us
    pallas_call x1, Pallas kernels, attend(): pl.pallas_call(attend_kernel, grid_spec=pltpu.PrefetchScalarGridSpec(num_...  11.8 us
    dot_general x1, matrix products, shards(): jnp.dot(gathered.reshape(-1, gathered.shape[2]), key_value_weight.reshape...  7.06 us
  transfers between devices with their start and end apart: 1, of which 1 were waited for; matrix products, arithmetic and copies ran while one was open for 3% of the time, Pallas kernels for 44%

profile of v1, /device:TPU:2, one launch (start us, length us, event | category | flops | bytes accessed | tf_op | source)
XLA Modules:
  0.0 178.0 jit_solution(8536798797783415810)
XLA Ops:
  6.5 0.0 all-gather.2.cloned.1.call-start
  6.5 0.7 all-gather.2.cloned.1.call-update
  7.3 1.5 reshape.28.x_ref
  8.8 0.1 lt.35
  8.8 0.9 select_reduce_fusion
  9.8 0.1 reshape.27
  9.8 0.8 lt.37
  10.6 0.1 lt.38
  10.7 0.7 lt.39
  11.5 0.0 copy-done.5
  11.5 0.4 reshape.26.q_ref
  11.9 0.0 copy-start.6
  11.9 0.1 fusion.4
  12.0 0.1 select_reduce_fusion.1.seg_of_group
  12.2 0.0 copy-done.3
  12.2 0.0 copy-start.1
  12.2 1.4 copy-done.1
  13.6 1.0 copy-done.2
  14.6 77.7 %exchange.1.delta_ref = bf16[16,32,1280]{2,1,0:T(8,128)(2,1)S(1)} custom-call(s32[32]{0:T(128)S(1)} %select_reduce_fusion.1.seg_of_group, s32[16]{0:T(128)S(1)} %dynamic-slice_bitcast_fusion.group_of_seg, s32[32]{0:T(128)S(1)} %get-tuple-element.5.local_of_replica, bf16[16,32,1024]{2,1,0:T(8,128)(2,1)S(1)} %reshape.28.x_ref, ...), custom_call_target="tpu_custom_call" | custom-call | flops 1000000000 | bytes 209715200 | tf_op jit(solution)/shard_map/exchange/pallas_call | solution.py:235
  92.3 45.6 %all-gather.2.cloned.1.call-done = bf16[256,2,8192]{2,1,0:T(2,128)(2,1)} async-done(((bf16[256,2,1024]{2,1,0:T(2,128)(2,1)}), bf16[256,2,8192]{2,1,0:T(2,128)(2,1)}) %all-gather.2.cloned.1.call-update) | async-done | bytes 8388624 | tf_op jit(solution)/shard_map/all_gather | solution.py:368
  138.0 13.1 %reshape.29 = bf16[512,8192]{1,0:T(8,128)(2,1)} reshape(bf16[256,2,8192]{2,1,0:T(2,128)(2,1)} %all-gather.2.cloned.1.call-done) | data formatting | bytes 16777216 | tf_op jit(solution)/shard_map/reshape | solution.py:370
  151.1 7.1 %fusion.base_ref = f32[512,256]{1,0:T(8,128)S(1)} fusion(bf16[512,8192]{1,0:T(8,128)(2,1)} %reshape.29, bf16[1024,8,2,128]{3,2,1,0:T(2,128)(2,1)} %bitcast.9), kind=kOutput, calls=%fused_computation | convolution fusion | flops 2147483648 | bytes 13107200 | tf_op jit(solution)/shard_map/dot_general | solution.py:369
  158.2 11.8 %attend.1 = bf16[512,1024]{1,0:T(8,128)(2,1)S(1)} custom-call(s32[16]{0:T(128)S(1)} %copy-done.4, bf16[512,1024]{1,0:T(8,128)(2,1)S(1)} %reshape.26.q_ref, bf16[16,32,1280]{2,1,0:T(8,128)(2,1)S(1)} %exchange.1.delta_ref, f32[512,256]{1,0:T(8,128)S(1)} %fusion.base_ref, bf16[256,2,32,128]{3,2,1,0:T(8,128)(2,1)S(1)} %copy-done, ...), custom_call_target="tpu_custom_call" | custom-call | tf_op jit(solution)/shard_map/attend/pallas_call | solution.py:311
  170.0 1.2 reshape.31
  (11 shorter events, 0.0 us)
Async XLA Ops:
  6.5 4.9 %copy-start.5 = (bf16[256,2,1024]{2,1,0:T(2,128)(2,1)S(1)}, bf16[256,2,1024]{2,1,0:T(2,128)(2,1)}, u32[]{:S(2)}) copy-start(bf16[256,2,1024]{2,1,0:T(2,128)(2,1)} %param.12) | copy-start | bytes 3145732
  6.5 5.6 %copy-start.3 = (bf16[4,2,64,128]{3,2,1,0:T(8,128)(2,1)S(1)}, bf16[4,2,64,128]{3,2,1,0:T(8,128)(2,1)}, u32[]{:S(2)}) copy-start(bf16[4,2,64,128]{3,2,1,0:T(8,128)(2,1)} %upkv_ref.1) | copy-start | bytes 393220
  6.5 131.4 %all-gather.2.cloned.1.call-start = ((), (), s32[]{:S(2)}) async-start(), calls=%async_computation | async-start | bytes 9437184 | tf_op jit(solution)/shard_map/all_gather | solution.py:368
  11.9 80.4 %copy-start.6 = (s32[16,2,256]{2,1,0:T(2,128)S(1)}, s32[16,2,256]{2,1,0:T(2,128)}, u32[]{:S(2)}) copy-start(s32[16,2,256]{2,1,0:T(2,128)} %lt.39) | copy-start | bytes 98308
  12.2 1.4 copy-start.1
  13.6 1.0 copy-start.2
  151.1 7.1 %copy-start = (bf16[256,2,32,128]{3,2,1,0:T(8,128)(2,1)S(1)}, bf16[256,2,32,128]{3,2,1,0:T(8,128)(2,1)}, u32[]{:S(2)}) copy-start(bf16[256,2,32,128]{3,2,1,0:T(8,128)(2,1)} %cache_ref.1) | copy-start | bytes 12582916
  151.1 7.1 %copy-start.4 = (s32[16]{0:T(128)S(1)}, s32[16]{0:T(128)}, u32[]{:S(2)}) copy-start(s32[16]{0:T(128)} %live.1) | copy-start | bytes 196
Sparse Core Ops, SparseCore 0:
  9.1 128.8 all-gather.1

commit v2 on v1

--- a/solution.py
+++ b/solution.py
@@ -54,12 +54,16 @@
 
 
 def exchange_kernel(
-    seg_of_group, group_of_seg, local_of_replica, x_ref, down_ref, upq_ref, upkv_ref, out_ref,
-    xs, xr, part, rs, ag, ds, dr,
+    seg_of_group, group_of_seg, local_of_replica, x_ref, down_ref, upq_ref, upkv_ref, wpart_ref,
+    out_ref, base_ref,
+    xs, xr, part, rs, ag, ds, dr, wall, right_out, right_in, left_out, left_in,
     x_send, x_recv, rs_send, rs_recv, ag_send, ag_recv, d_send, d_recv,
+    wz_send, wz_recv, w1_send, w1_recv, w2_send, w2_recv, w3_send, w3_recv,
+    right_send, right_recv, left_send, left_recv,
 ):
     me = lax.axis_index("replica")
     t = lax.axis_index("tensor")
+    y, x, core = me // 8, (me // 2) % 4, me % 2
 
     barrier = pltpu.get_barrier_semaphore()
 
@@ -101,6 +105,144 @@
             send_sem=ag_send.at[chunk, u], recv_sem=ag_recv.at[chunk, sender],
             device_id=(me, u), device_id_type=MESH,
         )
+
+    def wz_copy(u, sender):
+        half = sender // 4
+        i = jnp.where(half == 0, y, x)
+        j = jnp.where(half == 0, x, y)
+        return pltpu.make_async_remote_copy(
+            src_ref=wpart_ref.at[u], dst_ref=wall.at[half, core, i, j, sender % 4],
+            send_sem=wz_send.at[u], recv_sem=wz_recv.at[sender],
+            device_id=(me, u), device_id_type=MESH,
+        )
+
+    def along(axis, d):
+        if axis == 0:
+            return ((y + d) % 4) * 8 + x * 2 + core
+        return y * 8 + ((x + d) % 4) * 2 + core
+
+    def w1_copy(half, d):
+        piece = wall.at[0, core, y, x] if half == 0 else wall.at[1, core, x, y]
+        return pltpu.make_async_remote_copy(
+            src_ref=piece, dst_ref=piece, send_sem=w1_send.at[half, d], recv_sem=w1_recv.at[half, d],
+            device_id=(along(1 - half, d), t), device_id_type=MESH,
+        )
+
+    def w2_copy(half, d):
+        piece = wall.at[0, core, y] if half == 0 else wall.at[1, core, x]
+        return pltpu.make_async_remote_copy(
+            src_ref=piece, dst_ref=piece, send_sem=w2_send.at[half, d], recv_sem=w2_recv.at[half, d],
+            device_id=(along(half, d), t), device_id_type=MESH,
+        )
+
+    def w3_copy(half, d):
+        line = ((y if half == 0 else x) + 4 - d) % 4
+        return pltpu.make_async_remote_copy(
+            src_ref=wall.at[half, core, line], dst_ref=wall.at[half, core, line],
+            send_sem=w3_send.at[half, d], recv_sem=w3_recv.at[half, d],
+            device_id=(y * 8 + x * 2 + 1 - core, t), device_id_type=MESH,
+        )
+
+    def weight_z():
+        def send(i, _):
+            wz_copy((t + i) % TZ, t).start()
+            return 0
+
+        lax.fori_loop(1, TZ, send, 0)
+        half = t // 4
+        i = jnp.where(half == 0, y, x)
+        j = jnp.where(half == 0, x, y)
+        wall[half, core, i, j, t % 4] = wpart_ref[t]
+
+    def weight_first():
+        def wait(i, _):
+            wz_copy(t, (t + TZ - i) % TZ).wait_recv()
+            return 0
+
+        lax.fori_loop(1, TZ, wait, 0)
+        for d in (2, 1, 3):
+            for half in range(2):
+                w1_copy(half, d).start()
+
+    def weight_second():
+        for d in (1, 3, 2):
+            for half in range(2):
+                w1_copy(half, d).wait_recv()
+        for d in (2, 1, 3):
+            for half in range(2):
+                w2_copy(half, d).start()
+        for half in range(2):
+            w3_copy(half, 0).start()
+
+    def weight_third():
+        for d in (1, 3, 2):
+            for half in range(2):
+                w2_copy(half, d).wait_recv()
+                w3_copy(half, d).start()
+
+    def weight_done():
+        for d in (0, 1, 3, 2):
+            for half in range(2):
+                w3_copy(half, d).wait_recv()
+
+    def right_copy(s):
+        return pltpu.make_async_remote_copy(
+            src_ref=right_out.at[s], dst_ref=right_in.at[s],
+            send_sem=right_send.at[s], recv_sem=right_recv.at[s],
+            device_id=(me, (t + 1) % TZ), device_id_type=MESH,
+        )
+
+    def left_copy(s):
+        return pltpu.make_async_remote_copy(
+            src_ref=left_out.at[s], dst_ref=left_in.at[s],
+            send_sem=left_send.at[s], recv_sem=left_recv.at[s],
+            device_id=(me, (t + TZ - 1) % TZ), device_id_type=MESH,
+        )
+
+    tall = 256
+    tiles = base_ref.shape[0] // tall
+    segs_of_tile = tall // x_ref.shape[1]
+
+    def base_part(share, write):
+        def tile(i, _):
+            w = wall[share // 4, :, :, :, share % 4].reshape(x_ref.shape[2], base_ref.shape[1])
+            rows = x_ref[pl.ds(i * segs_of_tile, segs_of_tile)].reshape(tall, x_ref.shape[2])
+            write(pl.ds(i * tall, tall), jnp.dot(rows, w, preferred_element_type=jnp.float32))
+            return 0
+
+        lax.fori_loop(0, tiles, tile, 0)
+
+    def ring(s):
+        if s < 4:
+            def to_right(at, value):
+                if s > 0:
+                    value = value + right_in[s - 1, at].astype(jnp.float32)
+                right_out[s, at] = value.astype(jnp.bfloat16)
+
+            if s > 0:
+                right_copy(s - 1).wait_recv()
+            base_part((t + 4 - s) % TZ, to_right)
+            right_copy(s).start()
+        if s < 3:
+            def to_left(at, value):
+                if s > 0:
+                    value = value + left_in[s - 1, at].astype(jnp.float32)
+                left_out[s, at] = value.astype(jnp.bfloat16)
+
+            if s > 0:
+                left_copy(s - 1).wait_recv()
+            base_part((t + TZ - 3 + s) % TZ, to_left)
+            left_copy(s).start()
+
+    def ring_end():
+        def to_base(at, value):
+            base_ref[at] = (
+                value + right_in[3, at].astype(jnp.float32) + left_in[2, at].astype(jnp.float32)
+            )
+
+        left_copy(2).wait_recv()
+        right_copy(3).wait_recv()
+        base_part(t, to_base)
 
     for chunk in range(CHUNKS):
         def fill(j, _, chunk=chunk):
@@ -110,6 +252,7 @@
 
         lax.fori_loop(0, PER, fill, 0)
     pl.semaphore_wait(barrier, SLOTS - 1 + TZ - 1)
+    weight_z()
     for chunk in range(CHUNKS):
         def send(j, _, chunk=chunk):
             x_copy(chunk, j).start()
@@ -183,7 +326,9 @@
             dr[me] = deltas(0)
         lax.fori_loop(1 if chunk == 0 else 0, PER, one, 0)
 
+    weight_first()
     shrink_parts(0)
+    weight_second()
     shrink_parts(1)
     add_up(0)
     shrink_parts(2)
@@ -192,9 +337,16 @@
     shrink_parts(3)
     add_up(2)
     give_back(1)
+    weight_third()
     add_up(3)
     give_back(2)
+    weight_done()
+    ring(0)
     give_back(3)
+    ring(1)
+    ring(2)
+    ring(3)
+    ring_end()
 
     for chunk in range(CHUNKS):
         def settle(j, _, chunk=chunk):
@@ -224,19 +376,39 @@
 
         lax.fori_loop(1, TZ, settle_z, 0)
 
-
-def exchange(seg_of_group, group_of_seg, local_of_replica, x, down, upq, upkv):
+    def settle_w(i, _):
+        wz_copy((t + i) % TZ, t).wait_send()
+        return 0
+
+    lax.fori_loop(1, TZ, settle_w, 0)
+    for half in range(2):
+        for d in range(1, 4):
+            w1_copy(half, d).wait_send()
+            w2_copy(half, d).wait_send()
+        for d in range(4):
+            w3_copy(half, d).wait_send()
+    for s in range(4):
+        right_copy(s).wait_send()
+    for s in range(3):
+        left_copy(s).wait_send()
+
+
+def exchange(seg_of_group, group_of_seg, local_of_replica, x, down, upq, upkv, wpart):
     segs, rows, features = x.shape
     ranks = down.shape[1]
     columns = upq.shape[2] + 2 * upkv.shape[3]
+    kv = wpart.shape[2]
     smem = pl.BlockSpec(memory_space=pltpu.SMEM)
     vmem = pl.BlockSpec(memory_space=pltpu.VMEM)
     dma = pltpu.SemaphoreType.DMA
     return pl.pallas_call(
         exchange_kernel,
-        out_shape=jax.ShapeDtypeStruct((segs, rows, columns), jnp.bfloat16),
-        in_specs=[smem] * 3 + [vmem] * 4,
-        out_specs=vmem,
+        out_shape=(
+            jax.ShapeDtypeStruct((segs, rows, columns), jnp.bfloat16),
+            jax.ShapeDtypeStruct((segs * rows, kv), jnp.float32),
+        ),
+        in_specs=[smem] * 3 + [vmem] * 5,
+        out_specs=(vmem, vmem),
         scratch_shapes=[
             pltpu.VMEM((SLOTS, rows, features), jnp.bfloat16),
             pltpu.VMEM((SLOTS, rows, features), jnp.bfloat16),
@@ -245,16 +417,24 @@
             pltpu.VMEM((CHUNKS, TZ, rows, ranks), jnp.bfloat16),
             pltpu.VMEM((SLOTS, rows, columns), jnp.bfloat16),
             pltpu.VMEM((SLOTS, rows, columns), jnp.bfloat16),
+            pltpu.VMEM((2, 2, 4, 4, 4) + wpart.shape[1:], jnp.bfloat16),
+            pltpu.VMEM((4, segs * rows, kv), jnp.bfloat16),
+            pltpu.VMEM((4, segs * rows, kv), jnp.bfloat16),
+            pltpu.VMEM((3, segs * rows, kv), jnp.bfloat16),
+            pltpu.VMEM((3, segs * rows, kv), jnp.bfloat16),
             dma((SLOTS,)), dma((SLOTS,)),
             dma((CHUNKS, TZ)), dma((CHUNKS, TZ)), dma((CHUNKS, TZ)), dma((CHUNKS, TZ)),
             dma((SLOTS,)), dma((SLOTS,)),
+            dma((TZ,)), dma((TZ,)),
+            dma((2, 4)), dma((2, 4)), dma((2, 4)), dma((2, 4)), dma((2, 4)), dma((2, 4)),
+            dma((4,)), dma((4,)), dma((3,)), dma((3,)),
         ],
         compiler_params=pltpu.CompilerParams(
-            collective_id=0, has_side_effects=True, vmem_limit_bytes=40 * 2**20
+            collective_id=0, has_side_effects=True, vmem_limit_bytes=48 * 2**20
         ),
         cost_estimate=pl.CostEstimate(flops=10**9, bytes_accessed=200 * 2**20, transcendentals=0),
         name="exchange",
-    )(seg_of_group, group_of_seg, local_of_replica, x, down, upq, upkv)
+    )(seg_of_group, group_of_seg, local_of_replica, x, down, upq, upkv, wpart)
 
 
 def attend_kernel(live, q_ref, delta_ref, base_ref, cache_ref, bias_ref, out_ref):
@@ -365,16 +545,16 @@
     )
     local_of_replica = jnp.sum(jnp.where(group == me, local, 0), axis=1)
 
-    gathered = lax.all_gather(normed_token_input, "tensor", axis=2, tiled=True)
-    base_kv = jnp.dot(
-        gathered.reshape(-1, gathered.shape[2]),
-        key_value_weight.reshape(-1, 2 * kv_wide),
-        preferred_element_type=jnp.float32,
-    )
-    delta = exchange(
+    tensors = lax.axis_size("tensor")
+    y, x, core = me // 8, (me // 2) % 4, me % 2
+    place = core * 16 + jnp.where(lax.axis_index("tensor") < 4, y * 4 + x, x * 4 + y)
+    by_place = key_value_weight.reshape(tensors, replicas, -1, 2, kv_wide)
+    wpart = lax.dynamic_index_in_dim(by_place, place, 1, keepdims=False)
+    wpart = wpart.reshape(tensors, wpart.shape[1], 2 * kv_wide)
+    delta, base_kv = exchange(
         seg_of_group, group_of_seg, local_of_replica,
         normed_token_input.reshape(segs, requests * tokens // segs, features),
-        adapter_down_maps, query_up_maps, key_value_up_maps,
+        adapter_down_maps, query_up_maps, key_value_up_maps, wpart,
     )
     spots = jnp.arange(CTX, dtype=jnp.int32)
     bias = jnp.where(spots[None, :] < cache_length[:, None], 0.0, -jnp.inf).astype(jnp.float32)

time: 179 us -> 134 us (0.75)
  waiting for transfers between devices: 46.3 us -> 0 us
  Pallas kernels: 89.5 us -> 119 us
  between operations: 13.5 us -> 0.13 us
  matrix products: 7.06 us -> 0 us
  local copies, waits for them, and re-layouts: 20.4 us -> 13.8 us
    all_gather x1 -> x0, waiting for transfers between devices: 45.6 us -> none  [shards(): gathered = lax.all_gather(normed_token_input, 'tensor', axis=2, tiled=True)]
    pallas_call x1, Pallas kernels: 77.7 us -> 107 us  [exchange(): pl.pallas_call(exchange_kernel, out_shape=(jax.ShapeDtypeStruct((segs, ro...]
    reshape x1, local copies, waits for them, and re-layouts: 13.1 us -> 0.09 us  [shards(): wpart = wpart.reshape(tensors, wpart.shape[1], 2 * kv_wide)]
    dot_general x1 -> x0, matrix products: 7.06 us -> none  [shards(): jnp.dot(gathered.reshape(-1, gathered.shape[2]), key_value_weight.reshape...]
    unnamed x14 -> x15, local copies, waits for them, and re-layouts: 2.47 us -> 8.37 us
  transfers between devices with their start and end apart: 1 -> 0, of which waited for: 1 -> 0; matrix products, arithmetic and copies ran while one was open for 3% -> 0% of each run, Pallas kernels for 44% -> 0%
where the time goes in v2:
time: 134 us
  Pallas kernels  119 us (89%)
  local copies, waits for them, and re-layouts  13.8 us (10%)
    pallas_call x1, Pallas kernels, exchange(): pl.pallas_call(exchange_kernel, out_shape=(jax.ShapeDtypeStruct((segs, ro...  107 us
    pallas_call x1, Pallas kernels, attend(): pl.pallas_call(attend_kernel, grid_spec=pltpu.PrefetchScalarGridSpec(num_...  11.8 us
    unnamed x15, local copies, waits for them, and re-layouts  8.37 us

profile of v2, /device:TPU:2, one launch (start us, length us, event | category | flops | bytes accessed | tf_op | source)
XLA Modules:
  0.0 133.7 jit_solution(5335491306657284570)
XLA Ops:
  0.0 0.9 select_reduce_fusion
  0.9 0.1 lt.56
  1.0 0.1 reshape.28
  1.1 0.1 fusion.1
  1.2 0.1 select_reduce_fusion.1.seg_of_group
  1.4 0.8 lt.58
  2.1 0.1 lt.59
  2.2 0.1 lt.60
  2.4 0.0 copy-start.3
  2.4 1.0 dynamic-slice_bitcast_fusion
  3.4 0.1 reshape.31.wpart_ref
  3.5 1.5 %reshape.29.x_ref = bf16[16,32,1024]{2,1,0:T(8,128)(2,1)S(1)} reshape(bf16[256,2,1024]{2,1,0:T(2,128)(2,1)} %param.11) | data formatting | bytes 2097152 | tf_op jit(solution)/shard_map/reshape | solution.py:556
  5.0 0.0 copy-start.4
  5.0 1.4 %copy-done.4 = bf16[4,192,1024]{2,1,0:T(8,128)(2,1)S(1)} copy-done((bf16[4,192,1024]{2,1,0:T(8,128)(2,1)S(1)}, bf16[4,192,1024]{2,1,0:T(8,128)(2,1)}, u32[]{:S(2)}) %copy-start.4) | copy-done | bytes 1572888
  6.4 1.0 copy-done.5
  7.4 0.9 copy-done.6
  8.3 106.8 %exchange.1 = (bf16[16,32,1280]{2,1,0:T(8,128)(2,1)S(1)}, f32[512,256]{1,0:T(8,128)S(1)}) custom-call(s32[32]{0:T(128)S(1)} %select_reduce_fusion.1.seg_of_group, s32[16]{0:T(128)S(1)} %dynamic-slice_bitcast_fusion.1.group_of_seg, s32[32]{0:T(128)S(1)} %get-tuple-element.9.local_of_replica, bf16[16,32,1024]{2,1,0:T(8,128)(2,1)S(1)} %reshape.29.x_ref, ...), custom_call_target="tpu_custom_call" | custom-call | flops 1000000000 | bytes 209715200 | tf_op jit(solution)/shard_map/exchange/pallas_call | solution.py:404
  115.2 0.8 copy-done.1
  116.0 1.5 %reshape.27.q_ref = bf16[512,1024]{1,0:T(8,128)(2,1)S(1)} reshape(bf16[256,2,1024]{2,1,0:T(2,128)(2,1)} %param.12) | data formatting | bytes 2097152 | tf_op jit(solution)/shard_map/reshape | solution.py:562
  117.5 0.0 copy-start
  117.5 2.2 %copy-done = bf16[256,2,32,128]{3,2,1,0:T(8,128)(2,1)S(1)} copy-done((bf16[256,2,32,128]{3,2,1,0:T(8,128)(2,1)S(1)}, bf16[256,2,32,128]{3,2,1,0:T(8,128)(2,1)}, u32[]{:S(2)}) %copy-start) | copy-done | bytes 4194328
  119.7 1.0 copy-done.2
  120.7 11.8 %attend.1 = bf16[512,1024]{1,0:T(8,128)(2,1)S(1)} custom-call(s32[16]{0:T(128)S(1)} %copy-done.3, bf16[512,1024]{1,0:T(8,128)(2,1)S(1)} %reshape.27.q_ref, bf16[16,32,1280]{2,1,0:T(8,128)(2,1)S(1)} %get-tuple-element.7.delta_ref, f32[512,256]{1,0:T(8,128)S(1)} %copy-done.2, bf16[256,2,32,128]{3,2,1,0:T(8,128)(2,1)S(1)} %copy-done, ...), custom_call_target="tpu_custom_call" | custom-call | tf_op jit(solution)/shard_map/attend/pallas_call | solution.py:491
  132.5 1.2 reshape.32
  (8 shorter events, 0.0 us)
Async XLA Ops:
  2.4 115.1 %copy-start.3 = (s32[16]{0:T(128)S(1)}, s32[16]{0:T(128)}, u32[]{:S(2)}) copy-start(s32[16]{0:T(128)} %live.1) | copy-start | bytes 196
  5.0 1.4 %copy-start.4 = (bf16[4,192,1024]{2,1,0:T(8,128)(2,1)S(1)}, bf16[4,192,1024]{2,1,0:T(8,128)(2,1)}, u32[]{:S(2)}) copy-start(bf16[4,192,1024]{2,1,0:T(8,128)(2,1)} %down_ref.1) | copy-start | bytes 4718596
  6.4 1.0 copy-start.5
  7.4 0.9 copy-start.6
  115.2 0.8 copy-start.1
  117.5 2.2 %copy-start = (bf16[256,2,32,128]{3,2,1,0:T(8,128)(2,1)S(1)}, bf16[256,2,32,128]{3,2,1,0:T(8,128)(2,1)}, u32[]{:S(2)}) copy-start(bf16[256,2,32,128]{3,2,1,0:T(8,128)(2,1)} %cache_ref.1) | copy-start | bytes 12582916
  119.7 1.0 copy-start.2

commit v3 on v1

v3 whole, which is shorter than its diff:
```python
import functools
import math

import jax
import jax.numpy as jnp
from jax import lax
from jax.experimental import pallas as pl
from jax.experimental.pallas import tpu as pltpu
from jax.sharding import PartitionSpec as P

HEAD_WIDTH = 128
CTX = 32
ADAPTER_SCALE = 0.5
MESH = pl.DeviceIdType.MESH

RINGS = (
    ((2, 2),),
    ((2, 1), (1, 2), (2, 3), (3, 2)),
    ((0, 2), (2, 0)),
    ((1, 1), (3, 3), (1, 3), (3, 1)),
    ((0, 1), (1, 0), (0, 3), (3, 0)),
)
OFFSETS = [(0, 0, 0)] + [(dy, dx, dc) for ring in RINGS for dc in (0, 1) for dy, dx in ring] + [(0, 0, 1)]
SLOTS = 32
CHUNKS = 4
PER = SLOTS // CHUNKS
TZ = 8


def packed(chunk, which, bits):
    total = 0
    for j in range(PER):
        total += OFFSETS[chunk * PER + j][which] << (bits * j)
    return total


PACK_Y = [packed(c, 0, 2) for c in range(CHUNKS)]
PACK_X = [packed(c, 1, 2) for c in range(CHUNKS)]
PACK_C = [packed(c, 2, 1) for c in range(CHUNKS)]


def offset(chunk, j):
    return (
        (PACK_Y[chunk] >> (2 * j)) & 3,
        (PACK_X[chunk] >> (2 * j)) & 3,
        (PACK_C[chunk] >> j) & 1,
    )


def moved(me, off, sign):
    y, x, c = me // 8, (me // 2) % 4, me % 2
    dy, dx, dc = off
    return ((y + 4 + sign * dy) % 4) * 8 + ((x + 4 + sign * dx) % 4) * 2 + (c + dc) % 2


def layer_kernel(
    seg_of_group, group_of_seg, local_of_replica, live, lengths,
    x_hbm, down_hbm, upq_hbm, upkv_hbm, q_hbm, cache_hbm, wpart_ref,
    out_ref,
    x_raw, down_ref, upq_ref, upkv_ref, q_raw, cache_ref, load_sem,
    x_ref, q_ref, base_ref, res, same,
    xs, xr, part, rs, ag, ds, dr, wall, right_out, right_in, left_out, left_in,
    x_send, x_recv, rs_send, rs_recv, ag_send, ag_recv, d_send, d_recv,
    wz_send, wz_recv, wp_send, wp_recv, ws_send, ws_recv, own_sem,
    right_send, right_recv, left_send, left_recv,
):
    me = lax.axis_index("replica")
    t = lax.axis_index("tensor")
    y, x, core = me // 8, (me // 2) % 4, me % 2

    barrier = pltpu.get_barrier_semaphore()

    def greet_plane(i, _):
        pl.semaphore_signal(barrier, inc=1, device_id=((me + i) % SLOTS, t), device_id_type=MESH)
        return 0

    def greet_z(i, _):
        pl.semaphore_signal(barrier, inc=1, device_id=(me, (t + i) % TZ), device_id_type=MESH)
        return 0

    lax.fori_loop(1, SLOTS, greet_plane, 0)
    lax.fori_loop(1, TZ, greet_z, 0)

    loads = [
        pltpu.make_async_copy(src, dst, load_sem.at[i])
        for i, (src, dst) in enumerate(
            [(x_hbm, x_raw), (down_hbm, down_ref), (upq_hbm, upq_ref), (upkv_hbm, upkv_ref),
             (cache_hbm, cache_ref), (q_hbm, q_raw)]
        )
    ]
    for load in loads:
        load.start()

    def x_copy(chunk, j):
        p = chunk * PER + j
        return pltpu.make_async_remote_copy(
            src_ref=xs.at[p], dst_ref=xr.at[p], send_sem=x_send.at[p], recv_sem=x_recv.at[p],
            device_id=(moved(me, offset(chunk, j), 1), t), device_id_type=MESH,
        )

    def d_copy(chunk, j):
        p = chunk * PER + j
        return pltpu.make_async_remote_copy(
            src_ref=ds.at[p], dst_ref=dr.at[p], send_sem=d_send.at[p], recv_sem=d_recv.at[p],
            device_id=(moved(me, offset(chunk, j), -1), t), device_id_type=MESH,
        )

    def rs_copy(chunk, u, sender):
        return pltpu.make_async_remote_copy(
            src_ref=part.at[chunk * PER + u], dst_ref=rs.at[chunk, sender],
            send_sem=rs_send.at[chunk, u], recv_sem=rs_recv.at[chunk, sender],
            device_id=(me, u), device_id_type=MESH,
        )

    def ag_copy(chunk, u, sender):
        return pltpu.make_async_remote_copy(
            src_ref=ag.at[chunk, sender], dst_ref=ag.at[chunk, sender],
            send_sem=ag_send.at[chunk, u], recv_sem=ag_recv.at[chunk, sender],
            device_id=(me, u), device_id_type=MESH,
        )

    def pair_of(share):
        quarter = share // 2
        on_y = quarter // 2
        b = (jnp.where(on_y == 1, y, x) + quarter % 2) % 2
        step = 1 + 2 * b
        partner = jnp.where(
            on_y == 1, ((y + step) % 4) * 8 + x * 2 + core, y * 8 + ((x + step) % 4) * 2 + core
        )
        return b, partner

    def wz_copy(u, sender):
        return pltpu.make_async_remote_copy(
            src_ref=wpart_ref.at[u], dst_ref=wall.at[sender, core, pair_of(sender)[0]],
            send_sem=wz_send.at[u], recv_sem=wz_recv.at[sender],
            device_id=(me, u), device_id_type=MESH,
        )

    def wp_copy(u):
        b, partner = pair_of(u)
        piece = wall.at[u, core, b]
        return pltpu.make_async_remote_copy(
            src_ref=piece, dst_ref=piece, send_sem=wp_send.at[u], recv_sem=wp_recv.at[u],
            device_id=(partner, t), device_id_type=MESH,
        )

    def ws_copy(u, k):
        b = pair_of(u)[0]
        piece = wall.at[u, core, (b + k) % 2]
        return pltpu.make_async_remote_copy(
            src_ref=piece, dst_ref=piece, send_sem=ws_send.at[u, k], recv_sem=ws_recv.at[u, k],
            device_id=(y * 8 + x * 2 + 1 - core, t), device_id_type=MESH,
        )

    own_weight = pltpu.make_async_copy(
        wpart_ref.at[t], wall.at[t, core, pair_of(t)[0]], own_sem.at[0]
    )

    def weight_z():
        for d in (4, 3, 5, 2, 6, 1, 7):
            wz_copy((t + d) % TZ, t).start()
        own_weight.start()

    steps = ((4, 5), (3, 6), (2, 7), (1,), (0,))

    def weight_first(s):
        for d in steps[s]:
            u = (t + d) % TZ
            if d:
                wz_copy(t, u).wait_recv()
            else:
                own_weight.wait()
            wp_copy(u).start()
            ws_copy(u, 0).start()

    def weight_second(s):
        for d in steps[s]:
            u = (t + d) % TZ
            wp_copy(u).wait_recv()
            ws_copy(u, 1).start()

    def weight_third(s):
        for d in steps[s]:
            u = (t + d) % TZ
            ws_copy(u, 0).wait_recv()
            ws_copy(u, 1).wait_recv()

    tall = 256
    segs_of_tile = tall // x_ref.shape[1]
    tiles = x_ref.shape[0] // segs_of_tile

    def right_copy(s, i):
        at = pl.ds(i * tall, tall)
        return pltpu.make_async_remote_copy(
            src_ref=right_out.at[s, at], dst_ref=right_in.at[s, at],
            send_sem=right_send.at[s, i], recv_sem=right_recv.at[s, i],
            device_id=(me, (t + 1) % TZ), device_id_type=MESH,
        )

    def left_copy(s, i):
        at = pl.ds(i * tall, tall)
        return pltpu.make_async_remote_copy(
            src_ref=left_out.at[s, at], dst_ref=left_in.at[s, at],
            send_sem=left_send.at[s, i], recv_sem=left_recv.at[s, i],
            device_id=(me, (t + TZ - 1) % TZ), device_id_type=MESH,
        )

    def base_part(share, i):
        w = wall[share].reshape(x_ref.shape[2], base_ref.shape[2])
        rows = x_ref[pl.ds(i * segs_of_tile, segs_of_tile)].reshape(tall, x_ref.shape[2])
        return jnp.dot(rows, w, preferred_element_type=jnp.float32)

    def ring(s):
        def tile(i, _):
            at = pl.ds(i * tall, tall)
            if s < 4:
                value = base_part((t + 4 - s) % TZ, i)
                if s > 0:
                    right_copy(s - 1, i).wait_recv()
                    value = value + right_in[s - 1, at].astype(jnp.float32)
                right_out[s, at] = value.astype(jnp.bfloat16)
                right_copy(s, i).start()
            if s < 3:
                value = base_part((t + TZ - 3 + s) % TZ, i)
                if s > 0:
                    left_copy(s - 1, i).wait_recv()
                    value = value + left_in[s - 1, at].astype(jnp.float32)
                left_out[s, at] = value.astype(jnp.bfloat16)
                left_copy(s, i).start()
            return 0

        lax.fori_loop(0, tiles, tile, 0)

    def ring_end():
        def tile(i, _):
            at = pl.ds(i * tall, tall)
            value = base_part(t, i)
            left_copy(2, i).wait_recv()
            right_copy(3, i).wait_recv()
            value = value + right_in[3, at].astype(jnp.float32) + left_in[2, at].astype(jnp.float32)
            base_ref[pl.ds(i * segs_of_tile, segs_of_tile)] = value.reshape(
                segs_of_tile, base_ref.shape[1], base_ref.shape[2]
            )
            return 0

        lax.fori_loop(0, tiles, tile, 0)

    per_seg = x_raw.shape[0] // x_ref.shape[0]

    def by_rows(raw, ref):
        def one(s, _):
            ref[s] = raw[pl.ds(s * per_seg, per_seg)].reshape(ref.shape[1:])
            return 0

        lax.fori_loop(0, ref.shape[0], one, 0)

    loads[0].wait()
    by_rows(x_raw, x_ref)
    for chunk in range(CHUNKS):
        def fill(j, _, chunk=chunk):
            group = moved(me, offset(chunk, j), 1)
            xs[chunk * PER + j] = x_ref[seg_of_group[group]]
            return 0

        lax.fori_loop(0, PER, fill, 0)
    pl.semaphore_wait(barrier, SLOTS - 1 + TZ - 1)
    weight_z()

    def send_inputs(chunk):
        def send(j, _):
            x_copy(chunk, j).start()
            return 0

        lax.fori_loop(1 if chunk == 0 else 0, PER, send, 0)

    def shrink_parts(chunk):
        def one(j, _):
            p = chunk * PER + j
            rows = xs[0] if chunk == 0 and isinstance(j, int) else xr[p]
            w = down_ref[local_of_replica[moved(me, offset(chunk, j), -1)]]
            part[p] = lax.dot_general(
                rows, w, (((1,), (1,)), ((), ())), preferred_element_type=jnp.float32
            ).astype(jnp.bfloat16)
            return 0

        def arrived(j, _):
            x_copy(chunk, j).wait_recv()
            return one(j, 0)

        if chunk == 0:
            one(0, 0)
        lax.fori_loop(1 if chunk == 0 else 0, PER, arrived, 0)

        def send(i, _):
            rs_copy(chunk, (t + i) % TZ, t).start()
            return 0

        lax.fori_loop(1, TZ, send, 0)

    def add_up(chunk):
        def wait(i, _):
            rs_copy(chunk, t, (t + TZ - i) % TZ).wait_recv()
            return 0

        lax.fori_loop(1, TZ, wait, 0)
        rs[chunk, t] = part[chunk * PER + t]
        total = rs[chunk, 0].astype(jnp.float32)
        for u in range(1, TZ):
            total = total + rs[chunk, u].astype(jnp.float32)
        ag[chunk, t] = total.astype(jnp.bfloat16)

        def send(i, _):
            ag_copy(chunk, (t + i) % TZ, t).start()
            return 0

        lax.fori_loop(1, TZ, send, 0)

    def give_back(chunk):
        def wait(i, _):
            ag_copy(chunk, t, (t + TZ - i) % TZ).wait_recv()
            return 0

        lax.fori_loop(1, TZ, wait, 0)

        def deltas(j):
            a = local_of_replica[moved(me, offset(chunk, j), -1)]
            shrink = ag[chunk, j]
            q = jnp.dot(shrink[:, 0:64], upq_ref[a], preferred_element_type=jnp.float32)
            k = jnp.dot(shrink[:, 64:128], upkv_ref[a, 0], preferred_element_type=jnp.float32)
            v = jnp.dot(shrink[:, 128:192], upkv_ref[a, 1], preferred_element_type=jnp.float32)
            return jnp.concatenate([q, k, v], axis=1).astype(jnp.bfloat16)

        def one(j, _):
            ds[chunk * PER + j] = deltas(j)
            d_copy(chunk, j).start()
            return 0

        if chunk == 0:
            dr[0] = deltas(0)
        lax.fori_loop(1 if chunk == 0 else 0, PER, one, 0)

    half = 8
    heads = q_ref.shape[2] // HEAD_WIDTH
    wide = q_ref.shape[2]
    rows = half * 2
    n = heads * rows
    unit = math.log2(math.e) / math.sqrt(HEAD_WIDTH)

    old_keys = half * CTX
    all_keys = same.shape[1]

    def prepare():
        row = lax.broadcasted_iota(jnp.int32, same.shape, 0) % rows
        col = lax.broadcasted_iota(jnp.int32, same.shape, 1)
        new = col - old_keys
        old_fits = jnp.where(row // 2 == col // CTX, 0.0, -jnp.inf)
        new_fits = jnp.where((row // 2 == new // 2) & (new <= row), 0.0, -jnp.inf)
        same[...] = jnp.where(new < 0, old_fits, new_fits)
        loads[5].wait()
        by_rows(q_raw, q_ref)

    def attend(chunk):
        spot = lax.broadcasted_iota(jnp.int32, (1, old_keys), 1)
        owner, nth = spot // CTX, spot % CTX
        pad = jnp.zeros((all_keys - old_keys - rows, HEAD_WIDTH), jnp.bfloat16)
        ones = jnp.ones((all_keys, HEAD_WIDTH), jnp.bfloat16)
        no_bias = jnp.zeros((1, all_keys - old_keys), jnp.float32)

        def slot(j):
            group = moved(me, offset(chunk, j), 1)
            seg = seg_of_group[group]
            delta = dr[chunk * PER + j].astype(jnp.float32) * ADAPTER_SCALE
            q_all = (q_ref[seg].astype(jnp.float32) + delta[:, :wide]).astype(jnp.bfloat16)
            fresh = (base_ref[seg] + delta[:, wide:]).astype(jnp.bfloat16)
            outs = []
            for h in range(2):
                at = slice(h * rows, (h + 1) * rows)
                q = jnp.concatenate(
                    [q_all[at, g * HEAD_WIDTH : (g + 1) * HEAD_WIDTH] for g in range(heads)], axis=0
                )
                keys = cache_ref[seg, h * half : (h + 1) * half, 0].reshape(old_keys, HEAD_WIDTH)
                values = cache_ref[seg, h * half : (h + 1) * half, 1].reshape(old_keys, HEAD_WIDTH)
                keys = jnp.concatenate([keys, fresh[at, :HEAD_WIDTH], pad], axis=0)
                values = jnp.concatenate([values, fresh[at, HEAD_WIDTH:], pad], axis=0)
                values = jnp.concatenate([values, ones], axis=1)
                ends = jnp.zeros(spot.shape, jnp.int32)
                for i in range(half):
                    ends = jnp.where(owner == i, lengths[seg * 2 * half + h * half + i], ends)
                bias = jnp.concatenate([jnp.where(nth < ends, 0.0, -jnp.inf), no_bias], axis=1)
                scores = lax.dot_general(
                    q, keys, (((1,), (1,)), ((), ())), preferred_element_type=jnp.float32
                )
                scores = scores + (same[...] + bias)
                lifted = jnp.exp2((scores - jnp.max(scores, axis=1, keepdims=True)) * unit)
                mixed = jnp.dot(lifted.astype(jnp.bfloat16), values, preferred_element_type=jnp.float32)
                mixed = mixed[:, :HEAD_WIDTH] / mixed[:, HEAD_WIDTH:]
                out = jnp.concatenate(
                    [mixed[g * rows : (g + 1) * rows] for g in range(heads)], axis=1
                )
                place = h * half + lax.broadcasted_iota(jnp.int32, out.shape, 0) // 2
                outs.append(jnp.where(place < live[seg], out, 0.0).astype(jnp.bfloat16))
            return group, jnp.concatenate(outs, axis=0)

        def pair(i, _):
            for b in range(2):
                if chunk == 0 and b == 0:
                    @pl.when(i > 0)
                    def _():
                        d_copy(chunk, 2 * i).wait_recv()
                else:
                    d_copy(chunk, 2 * i + b).wait_recv()
            done = [slot(2 * i + b) for b in range(2)]
            for group, out in done:
                res[group] = out.reshape(res.shape[1:])
            return 0

        lax.fori_loop(0, PER // 2, pair, 0)

    send_inputs(0)
    send_inputs(1)
    prepare()
    loads[1].wait()
    shrink_parts(0)
    weight_first(0)
    send_inputs(2)
    send_inputs(3)
    loads[2].wait()
    loads[3].wait()
    weight_second(0)
    weight_first(1)
    add_up(0)
    weight_third(0)
    ring(0)
    shrink_parts(1)
    weight_second(1)
    weight_first(2)
    give_back(0)
    weight_third(1)
    ring(1)
    add_up(1)
    shrink_parts(2)
    weight_second(2)
    weight_first(3)
    weight_first(4)
    shrink_parts(3)
    add_up(2)
    give_back(1)
    weight_third(2)
    ring(2)
    weight_second(3)
    weight_second(4)
    add_up(3)
    give_back(2)
    weight_third(3)
    ring(3)
    give_back(3)
    weight_third(4)
    ring_end()
    loads[4].wait()
    for chunk in range(CHUNKS):
        attend(chunk)

    def gather(s, _):
        out_ref[pl.ds(s * per_seg, per_seg)] = res[group_of_seg[s]]
        return 0

    lax.fori_loop(0, x_ref.shape[0], gather, 0)

    for chunk in range(CHUNKS):
        def settle(j, _, chunk=chunk):
            x_copy(chunk, j).wait_send()
            d_copy(chunk, j).wait_send()
            return 0

        lax.fori_loop(1 if chunk == 0 else 0, PER, settle, 0)

        def settle_z(i, _, chunk=chunk):
            rs_copy(chunk, (t + i) % TZ, t).wait_send()
            ag_copy(chunk, (t + i) % TZ, t).wait_send()
            return 0

        lax.fori_loop(1, TZ, settle_z, 0)

    def settle_w(i, _):
        wz_copy((t + i) % TZ, t).wait_send()
        return 0

    lax.fori_loop(1, TZ, settle_w, 0)
    def settle_shares(u, _):
        wp_copy(u).wait_send()
        ws_copy(u, 0).wait_send()
        ws_copy(u, 1).wait_send()
        return 0

    lax.fori_loop(0, TZ, settle_shares, 0)

    def settle_ring(i, _):
        for s in range(4):
            right_copy(s, i).wait_send()
        for s in range(3):
            left_copy(s, i).wait_send()
        return 0

    lax.fori_loop(0, tiles, settle_ring, 0)


def layer(tables, x, down, upq, upkv, q, cache, wpart):
    segs = tables[1].shape[0]
    tokens, features = x.shape[1:]
    per_seg = x.shape[0] // segs
    rows = per_seg * tokens
    ranks = down.shape[1]
    kv = wpart.shape[2]
    wide = q.shape[2]
    columns = wide + kv
    smem = pl.BlockSpec(memory_space=pltpu.SMEM)
    vmem = pl.BlockSpec(memory_space=pltpu.VMEM)
    hbm = pl.BlockSpec(memory_space=pltpu.HBM)
    dma = pltpu.SemaphoreType.DMA
    tiles = segs * rows // 256
    half_rows = rows // 2 * (wide // HEAD_WIDTH)
    loaded = [x, down, upq, upkv, q, cache]

    def room(*shape, dtype=jnp.bfloat16):
        return pltpu.VMEM(shape, dtype)

    return pl.pallas_call(
        layer_kernel,
        out_shape=jax.ShapeDtypeStruct(q.shape, jnp.bfloat16),
        in_specs=[smem] * len(tables) + [hbm] * (len(loaded) + 1),
        out_specs=vmem,
        scratch_shapes=[room(*a.shape) for a in loaded]
        + [
            dma((len(loaded),)),
            room(segs, rows, features),
            room(segs, rows, wide),
            room(segs, rows, kv, dtype=jnp.float32),
            room(SLOTS, per_seg, tokens, wide),
            room(half_rows, rows // 4 * CTX + 128, dtype=jnp.float32),
            room(SLOTS, rows, features),
            room(SLOTS, rows, features),
            room(SLOTS, rows, ranks),
            room(CHUNKS, TZ, rows, ranks),
            room(CHUNKS, TZ, rows, ranks),
            room(SLOTS, rows, columns),
            room(SLOTS, rows, columns),
            room(TZ, 2, 2, *wpart.shape[1:]),
            room(4, segs * rows, kv),
            room(4, segs * rows, kv),
            room(3, segs * rows, kv),
            room(3, segs * rows, kv),
            dma((SLOTS,)), dma((SLOTS,)),
            dma((CHUNKS, TZ)), dma((CHUNKS, TZ)), dma((CHUNKS, TZ)), dma((CHUNKS, TZ)),
            dma((SLOTS,)), dma((SLOTS,)),
            dma((TZ,)), dma((TZ,)),
            dma((TZ,)), dma((TZ,)), dma((TZ, 2)), dma((TZ, 2)), dma((1,)),
            dma((4, tiles)), dma((4, tiles)), dma((3, tiles)), dma((3, tiles)),
        ],
        compiler_params=pltpu.CompilerParams(
            collective_id=0, has_side_effects=True, vmem_limit_bytes=52 * 2**20
        ),
        name="layer",
    )(*tables, *loaded, wpart)


def shards(
    normed_token_input,
    rotated_base_query,
    key_value_weight,
    key_value_cache,
    adapter_down_maps,
    query_up_maps,
    key_value_up_maps,
    adapter_storage_row,
    segment_adapter,
    segment_live_requests,
    cache_length,
):
    requests, tokens, features = normed_token_input.shape
    wide = rotated_base_query.shape[2]
    kv_wide = key_value_weight.shape[2]
    owned = adapter_down_maps.shape[0]
    replicas = lax.axis_size("replica")
    segs = segment_live_requests.shape[0]
    me = lax.axis_index("replica")

    adapter_ids = jnp.arange(adapter_storage_row.shape[0], dtype=jnp.int32)
    slot = jnp.sum(
        jnp.where(
            segment_adapter[:, None] == adapter_ids[None, :], adapter_storage_row[None, :], 0
        ),
        axis=1,
    ).reshape(replicas, segs)
    group, local = lax.div(slot, owned), lax.rem(slot, owned)
    group_of_seg = lax.dynamic_index_in_dim(group, me, 0, keepdims=False)
    group_ids = jnp.arange(replicas, dtype=jnp.int32)
    seg_ids = jnp.arange(segs, dtype=jnp.int32)
    seg_of_group = jnp.sum(
        jnp.where(group_of_seg[None, :] == group_ids[:, None], seg_ids[None, :], 0), axis=1
    )
    local_of_replica = jnp.sum(jnp.where(group == me, local, 0), axis=1)

    tensors = lax.axis_size("tensor")
    y, x, core = me // 8, (me // 2) % 4, me % 2
    quarter = lax.axis_index("tensor") // 2
    b = (jnp.where(quarter // 2 == 1, y, x) + quarter % 2) % 2
    by_place = key_value_weight.reshape(tensors, 4, -1, 2, kv_wide)
    wpart = lax.dynamic_index_in_dim(by_place, core * 2 + b, 1, keepdims=False)
    wpart = wpart.reshape(tensors, wpart.shape[1], 2 * kv_wide)
    return layer(
        (seg_of_group, group_of_seg, local_of_replica, segment_live_requests, cache_length),
        normed_token_input, adapter_down_maps, query_up_maps, key_value_up_maps,
        rotated_base_query,
        key_value_cache.reshape((segs, requests // segs) + key_value_cache.shape[1:]),
        wpart,
    )


def solution(mesh):
    return jax.shard_map(
        shards,
        mesh=mesh,
        in_specs=(
            P("replica", None, "tensor"),
            P("replica", None, "tensor"),
            P(None, None, "tensor"),
            P("replica", None, None, "tensor"),
            P("replica", None, "tensor"),
            P("replica", None, "tensor"),
            P("replica", None, None, "tensor"),
            P(),
            P(),
            P("replica"),
            P("replica"),
        ),
        out_specs=P("replica", None, "tensor"),
        check_vma=False,
    )
```

time: 179 us -> 110 us (0.61)
  the two profiles are of different devices: /device:TPU:2 before, /device:TPU:1 now
where the time goes in v3:
time: 110 us
  Pallas kernels  104 us (95%)
  local copies, waits for them, and re-layouts  4.52 us (4%)
  other arithmetic  1.28 us (1%)
    pallas_call x1, Pallas kernels, layer(): pl.pallas_call(layer_kernel, out_shape=jax.ShapeDtypeStruct(q.shape, jnp....  104 us
    unnamed x10, local copies, waits for them, and re-layouts  2.94 us

profile of v3, /device:TPU:1, one launch (start us, length us, event | category | flops | bytes accessed | tf_op | source)
XLA Modules:
  0.0 109.8 jit_solution(3941195296808093793)
XLA Ops:
  0.0 0.0 copy-start.2
  0.0 0.0 copy-start.3
  0.0 0.0 copy-start.1
  0.0 0.0 copy-start
  0.1 1.0 select_reduce_fusion
  1.2 0.1 reshape.17
  1.3 0.1 fusion.1
  1.4 0.1 select_reduce_fusion.1.seg_of_group
  1.5 2.0 %dynamic-slice_bitcast_fusion = bf16[8,1,256,2,128]{4,3,2,0,1:T(2,128)(2,1)S(1)} fusion(bf16[8,4,256,2,128]{4,3,2,1,0:T(2,128)(2,1)} %bitcast.9, s32[]{:T(128)S(6)} %select_n.68), kind=kLoop, calls=%fused_computation | loop fusion | bytes 2097156
  3.5 1.5 %reshape.21.wpart_ref = bf16[8,256,256]{2,1,0:T(8,128)(2,1)} reshape(bf16[8,1,256,2,128]{4,3,2,0,1:T(2,128)(2,1)S(1)} %dynamic-slice_bitcast_fusion) | data formatting | bytes 2097152 | tf_op jit(solution)/shard_map/reshape | solution.py:609
  5.0 0.0 copy-done.2
  5.0 0.0 copy-done.3
  5.0 0.0 copy-done.1
  5.0 0.0 copy-done
  5.0 103.8 %layer.1 = bf16[256,2,1024]{2,1,0:T(2,128)(2,1)S(1)} custom-call(s32[32]{0:T(128)S(1)} %select_reduce_fusion.1.seg_of_group, s32[16]{0:T(128)S(1)} %dynamic-slice_bitcast_fusion.1.group_of_seg, s32[32]{0:T(128)S(1)} %get-tuple-element.5.local_of_replica, s32[16]{0:T(128)S(1)} %copy-done.3, s32[256]{0:T(256)S(1)} %copy-done.2, bf16[256,2,1024]{2,1,0:T(2,128)(2,1)} %x_hbm.1, ...), custom_call_target="tpu_custom_call" | custom-call | tf_op jit(solution)/shard_map/layer/pallas_call | solution.py:527
  108.8 1.0 copy.17
  (1 shorter events, 0.0 us)
Async XLA Ops:
  0.0 5.0 %copy-start.2 = (s32[256]{0:T(256)S(1)}, s32[256]{0:T(256)}, u32[]{:S(2)}) copy-start(s32[256]{0:T(256)} %lengths.1) | copy-start | bytes 3076
  0.0 5.0 %copy-start.3 = (s32[16]{0:T(128)S(1)}, s32[16]{0:T(128)}, u32[]{:S(2)}) copy-start(s32[16]{0:T(128)} %live.1) | copy-start | bytes 196
  0.0 5.0 %copy-start.1 = (bf16[4,2,64,128]{3,2,1,0:T(8,128)(2,1)S(1)}, bf16[4,2,64,128]{3,2,1,0:T(8,128)(2,1)}, u32[]{:S(2)}) copy-start(bf16[4,2,64,128]{3,2,1,0:T(8,128)(2,1)} %upkv_hbm.1) | copy-start | bytes 393220
  0.0 5.0 %copy-start = (bf16[4,64,1024]{2,1,0:T(8,128)(2,1)S(1)}, bf16[4,64,1024]{2,1,0:T(8,128)(2,1)}, u32[]{:S(2)}) copy-start(bf16[4,64,1024]{2,1,0:T(8,128)(2,1)} %upq_hbm.1) | copy-start | bytes 1572868

commit v4 on v3

--- a/solution.py
+++ b/solution.py
@@ -55,11 +55,11 @@
 
 def layer_kernel(
     seg_of_group, group_of_seg, local_of_replica, live, lengths,
-    x_hbm, down_hbm, upq_hbm, upkv_hbm, q_hbm, cache_hbm, wpart_ref,
+    x_hbm, down_hbm, upq_hbm, upkv_hbm, q_hbm, cache_hbm, w_hbm,
     out_ref,
     x_raw, down_ref, upq_ref, upkv_ref, q_raw, cache_ref, load_sem,
-    x_ref, q_ref, base_ref, res, same,
-    xs, xr, part, rs, ag, ds, dr, wall, right_out, right_in, left_out, left_in,
+    x_ref, q_ref, base_ref, same,
+    xs, xr, part, rs, ag, ds, dr, wall, right_out, right_in, left_out, left_in, wnow,
     x_send, x_recv, rs_send, rs_recv, ag_send, ag_recv, d_send, d_recv,
     wz_send, wz_recv, wp_send, wp_recv, ws_send, ws_recv, own_sem,
     right_send, right_recv, left_send, left_recv,
@@ -101,7 +101,7 @@
     def d_copy(chunk, j):
         p = chunk * PER + j
         return pltpu.make_async_remote_copy(
-            src_ref=ds.at[p], dst_ref=dr.at[p], send_sem=d_send.at[p], recv_sem=d_recv.at[p],
+            src_ref=ds.at[p], dst_ref=dr.at[me], send_sem=d_send.at[p], recv_sem=d_recv.at[p],
             device_id=(moved(me, offset(chunk, j), -1), t), device_id_type=MESH,
         )
 
@@ -129,9 +129,13 @@
         )
         return b, partner
 
+    def own_rows(u):
+        place = core * 2 + pair_of(t)[0]
+        return w_hbm.at[pl.ds((u * 4 + place) * wall.shape[3], wall.shape[3])]
+
     def wz_copy(u, sender):
         return pltpu.make_async_remote_copy(
-            src_ref=wpart_ref.at[u], dst_ref=wall.at[sender, core, pair_of(sender)[0]],
+            src_ref=own_rows(u), dst_ref=wall.at[sender, core, pair_of(sender)[0]],
             send_sem=wz_send.at[u], recv_sem=wz_recv.at[sender],
             device_id=(me, u), device_id_type=MESH,
         )
@@ -153,15 +157,14 @@
         )
 
     own_weight = pltpu.make_async_copy(
-        wpart_ref.at[t], wall.at[t, core, pair_of(t)[0]], own_sem.at[0]
+        own_rows(t), wall.at[t, core, pair_of(t)[0]], own_sem.at[0]
     )
 
-    def weight_z():
-        for d in (4, 3, 5, 2, 6, 1, 7):
+    def weight_z(*hops):
+        for d in hops:
             wz_copy((t + d) % TZ, t).start()
-        own_weight.start()
-
-    steps = ((4, 5), (3, 6), (2, 7), (1,), (0,))
+
+    steps = ((4,), (3, 5), (2, 6), (1, 7), (0,))
 
     def weight_first(s):
         for d in steps[s]:
@@ -205,45 +208,52 @@
             device_id=(me, (t + TZ - 1) % TZ), device_id_type=MESH,
         )
 
-    def base_part(share, i):
-        w = wall[share].reshape(x_ref.shape[2], base_ref.shape[2])
+    def weight_of(share, k):
+        wide_rows = wall[share].reshape((x_ref.shape[2],) + wall.shape[4:])
+        wnow[k] = wide_rows.reshape(wnow.shape[1:])
+
+    def base_part(k, i):
         rows = x_ref[pl.ds(i * segs_of_tile, segs_of_tile)].reshape(tall, x_ref.shape[2])
-        return jnp.dot(rows, w, preferred_element_type=jnp.float32)
+        return jnp.dot(rows, wnow[k], preferred_element_type=jnp.float32)
+
+    def pass_right(s, i, value):
+        at = pl.ds(i * tall, tall)
+        if s > i:
+            right_copy(s - 1, i).wait_recv()
+            value = value + right_in[s - 1, at].astype(jnp.float32)
+        right_out[s, at] = value.astype(jnp.bfloat16)
+        right_copy(s, i).start()
+
+    def pass_left(s, i, value):
+        at = pl.ds(i * tall, tall)
+        if s > 1 - i:
+            left_copy(s - 1, i).wait_recv()
+            value = value + left_in[s - 1, at].astype(jnp.float32)
+        left_out[s, at] = value.astype(jnp.bfloat16)
+        left_copy(s, i).start()
 
     def ring(s):
-        def tile(i, _):
+        for k, d in enumerate(steps[s]):
+            weight_of((t + d) % TZ, k)
+        if s == 0:
+            pass_right(0, 0, base_part(0, 0))
+            pass_left(0, 1, base_part(0, 1))
+        else:
+            for i in range(tiles):
+                pass_right(s, i, base_part(0, i))
+                pass_left(s, i, base_part(1, i))
+
+    def ring_end():
+        weight_of(t, 0)
+        for i in range(tiles):
             at = pl.ds(i * tall, tall)
-            if s < 4:
-                value = base_part((t + 4 - s) % TZ, i)
-                if s > 0:
-                    right_copy(s - 1, i).wait_recv()
-                    value = value + right_in[s - 1, at].astype(jnp.float32)
-                right_out[s, at] = value.astype(jnp.bfloat16)
-                right_copy(s, i).start()
-            if s < 3:
-                value = base_part((t + TZ - 3 + s) % TZ, i)
-                if s > 0:
-                    left_copy(s - 1, i).wait_recv()
-                    value = value + left_in[s - 1, at].astype(jnp.float32)
-                left_out[s, at] = value.astype(jnp.bfloat16)
-                left_copy(s, i).start()
-            return 0
-
-        lax.fori_loop(0, tiles, tile, 0)
-
-    def ring_end():
-        def tile(i, _):
-            at = pl.ds(i * tall, tall)
-            value = base_part(t, i)
-            left_copy(2, i).wait_recv()
+            value = base_part(0, i)
+            left_copy(3, i).wait_recv()
             right_copy(3, i).wait_recv()
-            value = value + right_in[3, at].astype(jnp.float32) + left_in[2, at].astype(jnp.float32)
+            value = value + right_in[3, at].astype(jnp.float32) + left_in[3, at].astype(jnp.float32)
             base_ref[pl.ds(i * segs_of_tile, segs_of_tile)] = value.reshape(
                 segs_of_tile, base_ref.shape[1], base_ref.shape[2]
             )
-            return 0
-
-        lax.fori_loop(0, tiles, tile, 0)
 
     per_seg = x_raw.shape[0] // x_ref.shape[0]
 
@@ -264,7 +274,7 @@
 
         lax.fori_loop(0, PER, fill, 0)
     pl.semaphore_wait(barrier, SLOTS - 1 + TZ - 1)
-    weight_z()
+    own_weight.start()
 
     def send_inputs(chunk):
         def send(j, _):
@@ -272,15 +282,21 @@
             return 0
 
         lax.fori_loop(1 if chunk == 0 else 0, PER, send, 0)
+
+    def packed_shrink(shrink):
+        mid = shrink.shape[0] // 2
+        value = jnp.concatenate([shrink[:mid, 128:], shrink[mid:, 128:]], axis=1)
+        return jnp.concatenate([shrink[:, :128], value], axis=0)
 
     def shrink_parts(chunk):
         def one(j, _):
             p = chunk * PER + j
             rows = xs[0] if chunk == 0 and isinstance(j, int) else xr[p]
             w = down_ref[local_of_replica[moved(me, offset(chunk, j), -1)]]
-            part[p] = lax.dot_general(
+            shrink = lax.dot_general(
                 rows, w, (((1,), (1,)), ((), ())), preferred_element_type=jnp.float32
-            ).astype(jnp.bfloat16)
+            )
+            part[p] = packed_shrink(shrink).astype(jnp.bfloat16)
             return 0
 
         def arrived(j, _):
@@ -324,10 +340,13 @@
 
         def deltas(j):
             a = local_of_replica[moved(me, offset(chunk, j), -1)]
-            shrink = ag[chunk, j]
+            both = ag[chunk, j]
+            mid = both.shape[0] // 3
+            shrink, value = both[: 2 * mid], both[2 * mid :]
+            value = jnp.concatenate([value[:, :64], value[:, 64:]], axis=0)
             q = jnp.dot(shrink[:, 0:64], upq_ref[a], preferred_element_type=jnp.float32)
             k = jnp.dot(shrink[:, 64:128], upkv_ref[a, 0], preferred_element_type=jnp.float32)
-            v = jnp.dot(shrink[:, 128:192], upkv_ref[a, 1], preferred_element_type=jnp.float32)
+            v = jnp.dot(value, upkv_ref[a, 1], preferred_element_type=jnp.float32)
             return jnp.concatenate([q, k, v], axis=1).astype(jnp.bfloat16)
 
         def one(j, _):
@@ -336,7 +355,7 @@
             return 0
 
         if chunk == 0:
-            dr[0] = deltas(0)
+            dr[me] = deltas(0)
         lax.fori_loop(1 if chunk == 0 else 0, PER, one, 0)
 
     half = 8
@@ -359,17 +378,15 @@
         loads[5].wait()
         by_rows(q_raw, q_ref)
 
-    def attend(chunk):
+    def attend():
         spot = lax.broadcasted_iota(jnp.int32, (1, old_keys), 1)
         owner, nth = spot // CTX, spot % CTX
         pad = jnp.zeros((all_keys - old_keys - rows, HEAD_WIDTH), jnp.bfloat16)
         ones = jnp.ones((all_keys, HEAD_WIDTH), jnp.bfloat16)
         no_bias = jnp.zeros((1, all_keys - old_keys), jnp.float32)
 
-        def slot(j):
-            group = moved(me, offset(chunk, j), 1)
-            seg = seg_of_group[group]
-            delta = dr[chunk * PER + j].astype(jnp.float32) * ADAPTER_SCALE
+        def segment(seg):
+            delta = dr[group_of_seg[seg]].astype(jnp.float32) * ADAPTER_SCALE
             q_all = (q_ref[seg].astype(jnp.float32) + delta[:, :wide]).astype(jnp.bfloat16)
             fresh = (base_ref[seg] + delta[:, wide:]).astype(jnp.bfloat16)
             outs = []
@@ -399,23 +416,24 @@
                 )
                 place = h * half + lax.broadcasted_iota(jnp.int32, out.shape, 0) // 2
                 outs.append(jnp.where(place < live[seg], out, 0.0).astype(jnp.bfloat16))
-            return group, jnp.concatenate(outs, axis=0)
+            return jnp.concatenate(outs, axis=0).reshape((per_seg,) + out_ref.shape[1:])
 
         def pair(i, _):
-            for b in range(2):
-                if chunk == 0 and b == 0:
-                    @pl.when(i > 0)
-                    def _():
-                        d_copy(chunk, 2 * i).wait_recv()
-                else:
-                    d_copy(chunk, 2 * i + b).wait_recv()
-            done = [slot(2 * i + b) for b in range(2)]
-            for group, out in done:
-                res[group] = out.reshape(res.shape[1:])
-            return 0
-
-        lax.fori_loop(0, PER // 2, pair, 0)
-
+            outs = [segment(2 * i + k) for k in range(2)]
+            for k in range(2):
+                out_ref[pl.ds((2 * i + k) * per_seg, per_seg)] = outs[k]
+            return 0
+
+        lax.fori_loop(0, x_ref.shape[0] // 2, pair, 0)
+
+    def returned(chunk):
+        def wait(j, _):
+            d_copy(chunk, j).wait_recv()
+            return 0
+
+        lax.fori_loop(1 if chunk == 0 else 0, PER, wait, 0)
+
+    weight_z(4, 3, 5, 2, 6, 1, 7)
     send_inputs(0)
     send_inputs(1)
     prepare()
@@ -458,13 +476,8 @@
     ring_end()
     loads[4].wait()
     for chunk in range(CHUNKS):
-        attend(chunk)
-
-    def gather(s, _):
-        out_ref[pl.ds(s * per_seg, per_seg)] = res[group_of_seg[s]]
-        return 0
-
-    lax.fori_loop(0, x_ref.shape[0], gather, 0)
+        returned(chunk)
+    attend()
 
     for chunk in range(CHUNKS):
         def settle(j, _, chunk=chunk):
@@ -494,23 +507,21 @@
 
     lax.fori_loop(0, TZ, settle_shares, 0)
 
-    def settle_ring(i, _):
-        for s in range(4):
-            right_copy(s, i).wait_send()
-        for s in range(3):
-            left_copy(s, i).wait_send()
-        return 0
-
-    lax.fori_loop(0, tiles, settle_ring, 0)
-
-
-def layer(tables, x, down, upq, upkv, q, cache, wpart):
+    for s in range(4):
+        for i in range(tiles):
+            if s >= i:
+                right_copy(s, i).wait_send()
+            if s >= 1 - i:
+                left_copy(s, i).wait_send()
+
+
+def layer(tables, x, down, upq, upkv, q, cache, weight):
     segs = tables[1].shape[0]
     tokens, features = x.shape[1:]
     per_seg = x.shape[0] // segs
     rows = per_seg * tokens
-    ranks = down.shape[1]
-    kv = wpart.shape[2]
+    packed_rows = rows * down.shape[1] // HEAD_WIDTH
+    kv = weight.shape[1] * weight.shape[2]
     wide = q.shape[2]
     columns = wide + kv
     smem = pl.BlockSpec(memory_space=pltpu.SMEM)
@@ -535,32 +546,32 @@
             room(segs, rows, features),
             room(segs, rows, wide),
             room(segs, rows, kv, dtype=jnp.float32),
-            room(SLOTS, per_seg, tokens, wide),
             room(half_rows, rows // 4 * CTX + 128, dtype=jnp.float32),
             room(SLOTS, rows, features),
             room(SLOTS, rows, features),
-            room(SLOTS, rows, ranks),
-            room(CHUNKS, TZ, rows, ranks),
-            room(CHUNKS, TZ, rows, ranks),
+            room(SLOTS, packed_rows, HEAD_WIDTH),
+            room(CHUNKS, TZ, packed_rows, HEAD_WIDTH),
+            room(CHUNKS, TZ, packed_rows, HEAD_WIDTH),
             room(SLOTS, rows, columns),
             room(SLOTS, rows, columns),
-            room(TZ, 2, 2, *wpart.shape[1:]),
+            room(TZ, 2, 2, features // 4, *weight.shape[1:]),
             room(4, segs * rows, kv),
             room(4, segs * rows, kv),
-            room(3, segs * rows, kv),
-            room(3, segs * rows, kv),
+            room(4, segs * rows, kv),
+            room(4, segs * rows, kv),
+            room(2, features, kv),
             dma((SLOTS,)), dma((SLOTS,)),
             dma((CHUNKS, TZ)), dma((CHUNKS, TZ)), dma((CHUNKS, TZ)), dma((CHUNKS, TZ)),
             dma((SLOTS,)), dma((SLOTS,)),
             dma((TZ,)), dma((TZ,)),
             dma((TZ,)), dma((TZ,)), dma((TZ, 2)), dma((TZ, 2)), dma((1,)),
-            dma((4, tiles)), dma((4, tiles)), dma((3, tiles)), dma((3, tiles)),
+            dma((4, tiles)), dma((4, tiles)), dma((4, tiles)), dma((4, tiles)),
         ],
         compiler_params=pltpu.CompilerParams(
             collective_id=0, has_side_effects=True, vmem_limit_bytes=52 * 2**20
         ),
         name="layer",
-    )(*tables, *loaded, wpart)
+    )(*tables, *loaded, weight)
 
 
 def shards(
@@ -600,19 +611,12 @@
     )
     local_of_replica = jnp.sum(jnp.where(group == me, local, 0), axis=1)
 
-    tensors = lax.axis_size("tensor")
-    y, x, core = me // 8, (me // 2) % 4, me % 2
-    quarter = lax.axis_index("tensor") // 2
-    b = (jnp.where(quarter // 2 == 1, y, x) + quarter % 2) % 2
-    by_place = key_value_weight.reshape(tensors, 4, -1, 2, kv_wide)
-    wpart = lax.dynamic_index_in_dim(by_place, core * 2 + b, 1, keepdims=False)
-    wpart = wpart.reshape(tensors, wpart.shape[1], 2 * kv_wide)
     return layer(
         (seg_of_group, group_of_seg, local_of_replica, segment_live_requests, cache_length),
         normed_token_input, adapter_down_maps, query_up_maps, key_value_up_maps,
         rotated_base_query,
         key_value_cache.reshape((segs, requests // segs) + key_value_cache.shape[1:]),
-        wpart,
+        key_value_weight,
     )
 
 

time: 110 us -> 103 us (0.936)
  Pallas kernels: 104 us -> 97.7 us
    pallas_call x1, Pallas kernels: 104 us -> 97.7 us  [layer(): pl.pallas_call(layer_kernel, out_shape=jax.ShapeDtypeStruct(q.shape, jnp....]
    reshape x1 -> x0, local copies, waits for them, and re-layouts: 1.49 us -> none  [shards(): wpart = wpart.reshape(tensors, wpart.shape[1], 2 * kv_wide)]
    unnamed x10 -> x9, local copies, waits for them, and re-layouts: 2.94 us -> 4.25 us
where the time goes in v4:
time: 103 us
  Pallas kernels  97.7 us (95%)
  local copies, waits for them, and re-layouts  4.34 us (4%)
  other arithmetic  1.16 us (1%)
    pallas_call x1, Pallas kernels, layer(): pl.pallas_call(layer_kernel, out_shape=jax.ShapeDtypeStruct(q.shape, jnp....  97.7 us
    unnamed x9, local copies, waits for them, and re-layouts  4.25 us

profile of v4, /device:TPU:1, one launch (start us, length us, event | category | flops | bytes accessed | tf_op | source)
XLA Modules:
  0.0 103.3 jit_solution(13584960075995647418)
XLA Ops:
  0.0 0.9 select_reduce_fusion
  0.9 0.1 reshape.10
  1.0 0.1 fusion.1
  1.2 0.1 select_reduce_fusion.1.seg_of_group
  1.3 0.0 copy-start
  1.3 1.0 %copy-done = bf16[4,64,1024]{2,1,0:T(8,128)(2,1)S(1)} copy-done((bf16[4,64,1024]{2,1,0:T(8,128)(2,1)S(1)}, bf16[4,64,1024]{2,1,0:T(8,128)(2,1)}, u32[]{:S(2)}) %copy-start) | copy-done | bytes 524312
  2.3 0.0 copy-start.1
  2.3 0.9 copy-done.1
  3.2 0.0 copy-start.2
  3.2 0.7 copy-done.2
  3.9 0.0 copy-start.3
  3.9 0.7 copy-done.3
  4.6 97.7 %layer.1 = bf16[256,2,1024]{2,1,0:T(2,128)(2,1)S(1)} custom-call(s32[32]{0:T(128)S(1)} %select_reduce_fusion.1.seg_of_group, s32[16]{0:T(128)S(1)} %dynamic-slice_bitcast_fusion.group_of_seg, s32[32]{0:T(128)S(1)} %get-tuple-element.5.local_of_replica, s32[16]{0:T(128)S(1)} %copy-done.3, s32[256]{0:T(256)S(1)} %copy-done.2, bf16[256,2,1024]{2,1,0:T(2,128)(2,1)} %x_hbm.1, ...), custom_call_target="tpu_custom_call" | custom-call | tf_op jit(solution)/shard_map/layer/pallas_call | solution.py:538
  102.3 1.0 copy.13
  (1 shorter events, 0.0 us)
Async XLA Ops:
  1.3 1.0 %copy-start = (bf16[4,64,1024]{2,1,0:T(8,128)(2,1)S(1)}, bf16[4,64,1024]{2,1,0:T(8,128)(2,1)}, u32[]{:S(2)}) copy-start(bf16[4,64,1024]{2,1,0:T(8,128)(2,1)} %upq_hbm.1) | copy-start | bytes 1572868
  2.3 0.9 copy-start.1
  3.2 0.7 copy-start.2
  3.9 0.7 copy-start.3

commit v5 on v4

--- a/solution.py
+++ b/solution.py
@@ -433,12 +433,13 @@
 
         lax.fori_loop(1 if chunk == 0 else 0, PER, wait, 0)
 
-    weight_z(4, 3, 5, 2, 6, 1, 7)
+    weight_z(4, 3, 5)
     send_inputs(0)
     send_inputs(1)
     prepare()
     loads[1].wait()
     shrink_parts(0)
+    weight_z(2, 6, 1, 7)
     weight_first(0)
     send_inputs(2)
     send_inputs(3)

time: 103 us -> 101 us (0.981); the launches traced: 103 us -> 99.6 us
  Pallas kernels: 97.7 us -> 94 us
    pallas_call x1, Pallas kernels: 97.7 us -> 94 us  [layer(): pl.pallas_call(layer_kernel, out_shape=jax.ShapeDtypeStruct(q.shape, jnp....]
where the time goes in v5:
time: 101 us; the launch traced here: 99.6 us
  Pallas kernels  94 us (93%)
  local copies, waits for them, and re-layouts  4.34 us (4%)
  other arithmetic  1.16 us (1%)
    pallas_call x1, Pallas kernels, layer(): pl.pallas_call(layer_kernel, out_shape=jax.ShapeDtypeStruct(q.shape, jnp....  94 us
    unnamed x9, local copies, waits for them, and re-layouts  4.25 us

profile of v5, /device:TPU:1, one launch (start us, length us, event | category | flops | bytes accessed | tf_op | source)
XLA Modules:
  0.0 99.6 jit_solution(9032325448052296978)
XLA Ops:
  0.0 0.9 select_reduce_fusion
  0.9 0.1 reshape.10
  1.0 0.1 fusion.1
  1.2 0.1 select_reduce_fusion.1.seg_of_group
  1.3 0.0 copy-start
  1.3 1.0 %copy-done = bf16[4,64,1024]{2,1,0:T(8,128)(2,1)S(1)} copy-done((bf16[4,64,1024]{2,1,0:T(8,128)(2,1)S(1)}, bf16[4,64,1024]{2,1,0:T(8,128)(2,1)}, u32[]{:S(2)}) %copy-start) | copy-done | bytes 524312
  2.3 0.0 copy-start.1
  2.3 0.9 copy-done.1
  3.2 0.0 copy-start.2
  3.2 0.7 copy-done.2
  3.9 0.0 copy-start.3
  3.9 0.7 copy-done.3
  4.6 94.0 %layer.1 = bf16[256,2,1024]{2,1,0:T(2,128)(2,1)S(1)} custom-call(s32[32]{0:T(128)S(1)} %select_reduce_fusion.1.seg_of_group, s32[16]{0:T(128)S(1)} %dynamic-slice_bitcast_fusion.group_of_seg, s32[32]{0:T(128)S(1)} %get-tuple-element.5.local_of_replica, s32[16]{0:T(128)S(1)} %copy-done.3, s32[256]{0:T(256)S(1)} %copy-done.2, bf16[256,2,1024]{2,1,0:T(2,128)(2,1)} %x_hbm.1, ...), custom_call_target="tpu_custom_call" | custom-call | tf_op jit(solution)/shard_map/layer/pallas_call | solution.py:539
  98.6 1.0 copy.13
  (1 shorter events, 0.0 us)
Async XLA Ops:
  1.3 1.0 %copy-start = (bf16[4,64,1024]{2,1,0:T(8,128)(2,1)S(1)}, bf16[4,64,1024]{2,1,0:T(8,128)(2,1)}, u32[]{:S(2)}) copy-start(bf16[4,64,1024]{2,1,0:T(8,128)(2,1)} %upq_hbm.1) | copy-start | bytes 1572868
  2.3 0.9 copy-start.1
  3.2 0.7 copy-start.2
  3.9 0.7 copy-start.3

commit v6 on v5

--- a/solution.py
+++ b/solution.py
@@ -418,13 +418,13 @@
                 outs.append(jnp.where(place < live[seg], out, 0.0).astype(jnp.bfloat16))
             return jnp.concatenate(outs, axis=0).reshape((per_seg,) + out_ref.shape[1:])
 
-        def pair(i, _):
-            outs = [segment(2 * i + k) for k in range(2)]
-            for k in range(2):
-                out_ref[pl.ds((2 * i + k) * per_seg, per_seg)] = outs[k]
-            return 0
-
-        lax.fori_loop(0, x_ref.shape[0] // 2, pair, 0)
+        def four(i, _):
+            outs = [segment(4 * i + k) for k in range(4)]
+            for k in range(4):
+                out_ref[pl.ds((4 * i + k) * per_seg, per_seg)] = outs[k]
+            return 0
+
+        lax.fori_loop(0, x_ref.shape[0] // 4, four, 0)
 
     def returned(chunk):
         def wait(j, _):

time: 101 us -> 98.5 us (0.975)
  Pallas kernels: 94 us -> 91.8 us
    pallas_call x1, Pallas kernels: 94 us -> 91.8 us  [layer(): pl.pallas_call(layer_kernel, out_shape=jax.ShapeDtypeStruct(q.shape, jnp....]
where the time goes in v6:
time: 98.5 us; the launch traced here: 97.3 us
  Pallas kernels  91.8 us (93%)
  local copies, waits for them, and re-layouts  4.34 us (4%)
  other arithmetic  1.16 us (1%)
    pallas_call x1, Pallas kernels, layer(): pl.pallas_call(layer_kernel, out_shape=jax.ShapeDtypeStruct(q.shape, jnp....  91.8 us
    unnamed x9, local copies, waits for them, and re-layouts  4.25 us

profile of v6, /device:TPU:1, one launch (start us, length us, event | category | flops | bytes accessed | tf_op | source)
XLA Modules:
  0.0 97.3 jit_solution(941396956918796428)
XLA Ops:
  0.0 0.9 select_reduce_fusion
  0.9 0.1 reshape.10
  1.0 0.1 fusion.1
  1.2 0.1 select_reduce_fusion.1.seg_of_group
  1.3 0.0 copy-start
  1.3 1.0 %copy-done = bf16[4,64,1024]{2,1,0:T(8,128)(2,1)S(1)} copy-done((bf16[4,64,1024]{2,1,0:T(8,128)(2,1)S(1)}, bf16[4,64,1024]{2,1,0:T(8,128)(2,1)}, u32[]{:S(2)}) %copy-start) | copy-done | bytes 524312
  2.3 0.0 copy-start.1
  2.3 0.9 copy-done.1
  3.2 0.0 copy-start.2
  3.2 0.7 copy-done.2
  3.9 0.0 copy-start.3
  3.9 0.7 copy-done.3
  4.6 91.8 %layer.1 = bf16[256,2,1024]{2,1,0:T(2,128)(2,1)S(1)} custom-call(s32[32]{0:T(128)S(1)} %select_reduce_fusion.1.seg_of_group, s32[16]{0:T(128)S(1)} %dynamic-slice_bitcast_fusion.group_of_seg, s32[32]{0:T(128)S(1)} %get-tuple-element.5.local_of_replica, s32[16]{0:T(128)S(1)} %copy-done.3, s32[256]{0:T(256)S(1)} %copy-done.2, bf16[256,2,1024]{2,1,0:T(2,128)(2,1)} %x_hbm.1, ...), custom_call_target="tpu_custom_call" | custom-call | tf_op jit(solution)/shard_map/layer/pallas_call | solution.py:539
  96.3 1.0 copy.13
  (1 shorter events, 0.0 us)
Async XLA Ops:
  1.3 1.0 %copy-start = (bf16[4,64,1024]{2,1,0:T(8,128)(2,1)S(1)}, bf16[4,64,1024]{2,1,0:T(8,128)(2,1)}, u32[]{:S(2)}) copy-start(bf16[4,64,1024]{2,1,0:T(8,128)(2,1)} %upq_hbm.1) | copy-start | bytes 1572868
  2.3 0.9 copy-start.1
  3.2 0.7 copy-start.2
  3.9 0.7 copy-start.3
